TPU v7x, 256 devices: a whole 4x4x8 slice. The times are simulated.
256 devices in a mesh: rows: 32 (over x, z_lo, core), cols: 8 (over y, z_hi).
Axes of the slice: x: 4, y: 4, z: 8 (z_hi: 2, z_lo: 4; z = z_hi * 4 + z_lo), core: 2. Of those that a mesh axis runs over, the one named last changes fastest.
Arguments:
- density: float32 [8, 1024, 1024], P('cols', 'rows'), may hold values from 0.5 to 2
- velocity: float32 [3, 8, 1024, 1024], P(None, 'cols', 'rows'), may hold values from -2.5 to 2.5
- pressure: float32 [8, 1024, 1024], P('cols', 'rows'), may hold values from 0.5 to 36
- offsets_x: int32 [8, 1024], P('cols', 'rows'), may hold values from -2 to 2
- offsets_y: int32 [8, 1024], P('cols'), may hold values from -2 to 2
Outputs:
- density_out: float32 [8, 1024, 1024], P('cols', 'rows')
- velocity_out: float32 [3, 8, 1024, 1024], P(None, 'cols', 'rows')
- pressure_out: float32 [8, 1024, 1024], P('cols', 'rows')
All inputs are finite; a program needn't handle non-finite values.
Results may differ from a plain program's by a relative error of at most 0.0003.
Values sent between devices are 32-bit elements; how exact they have to be, the bound alone decides.
No kernel may reach another device: no remote copies, remote signals or barrier semaphores. Data moves between devices by JAX's collectives and lax.ppermute only.
A program may use at most 64 MiB of HBM per device.

v0:
```python
import jax
import jax.numpy as jnp
from jax import lax
from jax.experimental import pallas as pl
from jax.experimental.pallas import tpu as pltpu
from jax.sharding import PartitionSpec as P

SHIFT = 2
HALO = 8
LANES = 128
SUB = 8

courant = 0.4
adiabatic = 5.0 / 3.0


def clamp(v, a, b):
    return jnp.minimum(jnp.maximum(v, jnp.minimum(a, b)), jnp.maximum(a, b))


def face_of(am, a0, a1, a2):
    face = 7.0 / 12.0 * (a0 + a1) - 1.0 / 12.0 * (am + a2)
    return clamp(face, a0, a1)


def edges_of(a, face_before, face):
    triple = 3.0 * a
    low = clamp(face_before, a, triple - 2.0 * face)
    high = clamp(face, a, triple - 2.0 * face_before)
    return low, high


def sound_impedance(rho, inv_rho, p):
    return rho * jnp.sqrt(adiabatic * p * inv_rho)


def riemann(z, zn, u_right, u_left, p_right, p_left):
    inv = 1.0 / (z + zn)
    us = (z * u_right + zn * u_left + p_right - p_left) * inv
    ps = (zn * p_right + z * p_left + z * zn * (u_right - u_left)) * inv
    return us, ps


def total_energy(inv_rho, p, un, ta, tb):
    return p * inv_rho * (1.0 / (adiabatic - 1.0)) + 0.5 * (un * un + ta * ta + tb * tb)


def flux_weights(d, f):
    rest = 1.0 - f
    df = d * f
    return d * rest * rest, df * (3.0 - 2.0 * f), df * rest


def primitive(mass, mn, ma, mb, energy):
    inv = 1.0 / mass
    kinetic = 0.5 * (mn * mn + ma * ma + mb * mb) * inv
    return mass, mn * inv, ma * inv, mb * inv, (adiabatic - 1.0) * (energy - kinetic)


def roll_x(v, k):
    return pltpu.roll(v, k % v.shape[1], 1)


def profile_x(a):
    nxt = roll_x(a, -1)
    face = face_of(roll_x(a, 1), a, nxt, roll_x(a, -2))
    low, high = edges_of(a, roll_x(face, 1), face)
    return nxt, low, high


def speed_kernel(den, vel, prs, offx, pay, up, down, row):
    n_rows = den.shape[1]
    peak = None
    for g in range(n_rows // SUB):
        r = pl.ds(g * SUB, SUB)
        c = jnp.sqrt(adiabatic * prs[0, r, :] / den[0, r, :])
        s = jnp.maximum(jnp.abs(vel[0, 0, r, :]), jnp.abs(vel[1, 0, r, :])) + c
        peak = s if peak is None else jnp.maximum(peak, s)
    tile = peak[:, :LANES]
    for k in range(1, peak.shape[1] // LANES):
        tile = jnp.maximum(tile, peak[:, k * LANES : (k + 1) * LANES])
    line = jnp.max(tile, axis=0, keepdims=True)
    line = jnp.maximum(line, pltpu.roll(line, LANES // 2, 1))
    row[...] = jnp.broadcast_to(line, row.shape)
    row[0:1, 0:n_rows] = offx[...].astype(jnp.float32)
    pay[...] = jnp.broadcast_to(row[0:1, :], pay.shape)
    last = pl.ds(n_rows - HALO, HALO)
    first = pl.ds(0, HALO)
    for f, ref in enumerate((den, None, None, None, prs)):
        up[f] = ref[0, last, :] if ref is not None else vel[f - 1, 0, last, :]
        down[f] = ref[0, first, :] if ref is not None else vel[f - 1, 0, first, :]


def face_kernel(den, vel, prs, before, after, state):
    groups = den.shape[1] // SUB + 2
    for g in range(groups):
        if g == 0 or g == groups - 1:
            ref = before if g == 0 else after
            rho, un, ta, tb, p = (ref[f] for f in range(5))
        else:
            r = pl.ds((g - 1) * SUB, SUB)
            rho, p = den[0, r, :], prs[0, r, :]
            un, ta, tb = (vel[f, 0, r, :] for f in range(3))
        inv = 1.0 / rho
        z = sound_impedance(rho, inv, p)
        _, u_low, u_high = profile_x(un)
        _, p_low, p_high = profile_x(p)
        us, ps = riemann(z, roll_x(z, -1), u_high, roll_x(u_low, -1), p_high, roll_x(p_low, -1))
        work = us * ps
        o = pl.ds(g * SUB, SUB)
        state[0, o, :] = rho
        state[1, o, :] = us
        state[2, o, :] = us - roll_x(us, 1)
        state[3, o, :] = un
        state[4, o, :] = (ps - roll_x(ps, 1)) * inv
        state[5, o, :] = ta
        state[6, o, :] = tb
        state[7, o, :] = total_energy(inv, p, un, ta, tb)
        state[8, o, :] = (work - roll_x(work, 1)) * inv


def sweep_kernel(
    n_dev, n_cols, state, got, offy, den_out, vel_out, prs_out,
    pick, pick_s, offy8, swept, rows_out, tiles_out, pick_sem, out_sem,
):
    n_rows, n_x = den_out.shape[1:]
    n_tiles = n_x // LANES
    groups = n_rows // SUB + 2
    me, col = lax.axis_index("rows"), lax.axis_index("cols")
    for k, turn in enumerate((n_dev - 1, 0, 1)):
        pick[k : k + 1, :] = got[pl.ds(lax.rem(me + turn, n_dev) * n_cols + col, 1), :]
    pick_copy = pltpu.make_async_copy(pick, pick_s, pick_sem)
    pick_copy.start()
    for k in range(n_tiles):
        offy8[k : k + 1, :] = offy[:, k * LANES : (k + 1) * LANES]
    lane = lax.broadcasted_iota(jnp.int32, (SUB, LANES), 1)
    top = got[0:SUB, :]
    for k in range(1, got.shape[0] // SUB):
        top = jnp.maximum(top, got[k * SUB : (k + 1) * SUB, :])
    top = jnp.where(lane >= n_rows, top, 0.0)
    dt = courant / jnp.max(jnp.max(top, axis=0, keepdims=True), axis=1, keepdims=True)

    def x_group(g, carry):
        o = pl.ds(pl.multiple_of(g * SUB, SUB), SUB)
        rho, us, dus, un, gp, ta, tb, e, gw = (state[k, o, :] for k in range(9))
        w = 1.0 + dt * dus
        inv_w = 1.0 / w
        up = us > 0.0
        d = dt * us
        k1, k2, k3 = flux_weights(d, jnp.abs(d) * jnp.where(up, inv_w, roll_x(inv_w, -1)))
        lag = rho * inv_w
        contents = []
        for q in (lag, lag * (un - dt * gp), lag * ta, lag * tb, lag * (e - dt * gw)):
            nxt, low, high = profile_x(q)
            near = jnp.where(up, high, roll_x(low, -1))
            far = jnp.where(up, low, roll_x(high, -1))
            flux = k1 * near + k2 * jnp.where(up, q, nxt) - k3 * far
            contents.append(q * w + roll_x(flux, 1) - flux)
        for f, v in enumerate(primitive(*contents)):
            for k in range(n_tiles):
                at = pl.multiple_of((g * n_tiles + k) * SUB, SUB)
                swept[f, pl.ds(at, SUB), :] = v[:, k * LANES : (k + 1) * LANES]
        return carry

    lax.fori_loop(0, groups, x_group, 0)
    pick_copy.wait()

    total = groups * SUB

    def load_row(r):
        if r < HALO:
            s = pick_s[0, n_rows - HALO + r]
        elif r < HALO + n_rows:
            s = pick_s[1, r - HALO]
        else:
            s = pick_s[2, r - HALO - n_rows]
        s = s.astype(jnp.int32)
        turn = lax.rem(s + LANES, LANES)
        step = jnp.where(s > 0, 1, SUB - 1)
        over = lax.shift_right_arithmetic(lane - s, 7) != 0
        fields = []
        for f in range(5):
            at = (r // SUB) * n_tiles * SUB + r % SUB
            v = swept[f, pl.ds(at, SUB, stride=SUB), :]
            v = pltpu.roll(v, turn, 1)
            fields.append(jnp.where(over, pltpu.roll(v, step, 0), v))
        rho, ta, un, tb, p = fields
        return rho, un, ta, tb, p

    oy = offy8[...]
    moved = {k: oy == k for k in range(-SHIFT, SHIFT + 1) if k}
    cells, inv_rho, imp, faces, edges = {}, {}, {}, {}, {}
    stars, lags, weights, q_faces, q_edges, fluxes, done = {}, {}, {}, {}, {}, {}, {}
    copies = []
    for r in range(total):
        cells[r] = load_row(r)
        rho, un, ta, tb, p = cells[r]
        inv_rho[r] = 1.0 / rho
        imp[r] = sound_impedance(rho, inv_rho[r], p)
        i = r - 2
        if i >= 1:
            faces[i] = [face_of(*(cells[i + k][f] for k in (-1, 0, 1, 2))) for f in (1, 4)]
        if i >= 2:
            edges[i] = [edges_of(cells[i][f], faces[i - 1][n], faces[i][n]) for n, f in enumerate((1, 4))]
        i = r - 3
        if i >= 2:
            (_, u_right), (_, p_right) = edges[i]
            (u_left, _), (p_left, _) = edges[i + 1]
            us, ps = riemann(imp[i], imp[i + 1], u_right, u_left, p_right, p_left)
            stars[i] = us, ps, us * ps, dt * us
        if i >= 3:
            rho, un, ta, tb, p = cells[i]
            us, ps, work, d = stars[i]
            _, ps_b, work_b, d_b = stars[i - 1]
            w = 1.0 + d - d_b
            inv_w = 1.0 / w
            rate = dt * inv_rho[i]
            lag = rho * inv_w
            e = total_energy(inv_rho[i], p, un, ta, tb)
            lags[i] = (
                lag, lag * (un - rate * (ps - ps_b)), lag * ta, lag * tb, lag * (e - rate * (work - work_b)),
            )
            weights[i] = w, inv_w
        i = r - 5
        if i >= 4:
            q_faces[i] = [face_of(*(lags[i + k][f] for k in (-1, 0, 1, 2))) for f in range(5)]
        if i >= 5:
            q_edges[i] = [edges_of(lags[i][f], q_faces[i - 1][f], q_faces[i][f]) for f in range(5)]
        i = r - 6
        if i >= 5:
            d = stars[i][3]
            up = d > 0.0
            f_up = jnp.abs(d) * jnp.where(up, weights[i][1], weights[i + 1][1])
            k1, k2, k3 = flux_weights(d, f_up)
            fluxes[i] = []
            for f in range(5):
                low, high = q_edges[i][f]
                low_n, high_n = q_edges[i + 1][f]
                near = jnp.where(up, high, low_n)
                far = jnp.where(up, low, high_n)
                fluxes[i].append(k1 * near + k2 * jnp.where(up, lags[i][f], lags[i + 1][f]) - k3 * far)
        if i >= 6:
            done[i] = primitive(
                *(lags[i][f] * weights[i][0] + fluxes[i - 1][f] - fluxes[i][f] for f in range(5))
            )
        i = r - 8
        if i >= HALO:
            j = i - HALO
            a, b = divmod(j, SUB)
            for f in range(5):
                v = done[i][f]
                for k, mask in moved.items():
                    v = jnp.where(mask, done[i - k][f], v)
                rows_out[f, pl.ds(a * n_tiles * SUB + b, SUB, stride=SUB), :] = v
            if b == SUB - 1:
                for f, ref in enumerate(
                    (den_out.at[0], vel_out.at[1, 0], vel_out.at[0, 0], vel_out.at[2, 0], prs_out.at[0])
                ):
                    here = pl.ds(a * SUB, SUB)
                    for k in range(n_tiles):
                        tiles_out[f, here, pl.ds(k * LANES, LANES)] = rows_out[
                            f, pl.ds((a * n_tiles + k) * SUB, SUB), :
                        ]
                    copies.append(
                        pltpu.make_async_copy(tiles_out.at[f, here, :], ref.at[here, :], out_sem.at[f, a])
                    )
                    copies[-1].start()
    for copy in copies:
        copy.wait()


def body(n_dev, n_cols, density, velocity, pressure, offsets_x, offsets_y):
    n_rows, n_x = density.shape[1:]
    f32 = jnp.float32
    vmem = pl.BlockSpec(memory_space=pltpu.VMEM)
    everyone = n_dev * n_cols
    halo = jax.ShapeDtypeStruct((5, HALO, n_x), f32)
    pay, up, down = pl.pallas_call(
        speed_kernel,
        out_shape=(jax.ShapeDtypeStruct((everyone, LANES), f32), halo, halo),
        in_specs=[vmem] * 4,
        out_specs=[vmem] * 3,
        scratch_shapes=[pltpu.VMEM((SUB, LANES), f32)],
    )(density, velocity, pressure, offsets_x)
    got = lax.all_to_all(pay, ("rows", "cols"), split_axis=0, concat_axis=0, tiled=True)
    before = lax.ppermute(up, "rows", [(i, (i + 1) % n_dev) for i in range(n_dev)])
    after = lax.ppermute(down, "rows", [(i, (i - 1) % n_dev) for i in range(n_dev)])
    total = n_rows + 2 * HALO
    state = pl.pallas_call(
        face_kernel,
        out_shape=jax.ShapeDtypeStruct((9, total, n_x), f32),
        in_specs=[vmem] * 5,
        out_specs=vmem,
        cost_estimate=pl.CostEstimate(flops=total * n_x * 200, bytes_accessed=total * n_x * 64, transcendentals=0),
    )(density, velocity, pressure, before, after)
    plane = jax.ShapeDtypeStruct(density.shape, f32)
    any_space = pl.BlockSpec(memory_space=pl.ANY)
    tall = total * n_x // LANES
    short = n_rows * n_x // LANES
    return pl.pallas_call(
        lambda *refs: sweep_kernel(n_dev, n_cols, *refs),
        out_shape=(plane, jax.ShapeDtypeStruct(velocity.shape, f32), plane),
        in_specs=[vmem] * 3,
        out_specs=[any_space] * 3,
        scratch_shapes=[
            pltpu.VMEM((SUB, LANES), f32),
            pltpu.SMEM((SUB, LANES), f32),
            pltpu.VMEM((n_x // LANES, LANES), jnp.int32),
            pltpu.VMEM((5, tall, LANES), f32),
            pltpu.VMEM((5, short, LANES), f32),
            pltpu.VMEM((5, n_rows, n_x), f32),
            pltpu.SemaphoreType.DMA,
            pltpu.SemaphoreType.DMA((5, n_rows // SUB)),
        ],
    )(state, got, offsets_y)


def solution(mesh):
    n_dev, n_cols = mesh.shape["rows"], mesh.shape["cols"]
    return jax.shard_map(
        lambda *arrays: body(n_dev, n_cols, *arrays),
        mesh=mesh,
        in_specs=(
            P("cols", "rows", None),
            P(None, "cols", "rows", None),
            P("cols", "rows", None),
            P("cols", "rows"),
            P("cols", None),
        ),
        out_specs=(P("cols", "rows", None), P(None, "cols", "rows", None), P("cols", "rows", None)),
        check_vma=False,
    )
```

profile of v0, /device:TPU:8, one launch (start us, length us, event | category | flops | bytes accessed | tf_op | source)
XLA Modules:
  0.0 42.4 jit_solution(4408209992197019754)
XLA Ops:
  0.6 1.9 %shard_map.76 = (f32[256,128]{1,0:T(8,128)}, f32[5,8,1024]{2,1,0:T(8,128)}, f32[5,8,1024]{2,1,0:T(8,128)}) custom-call(f32[1,32,1024]{2,1,0:T(8,128)} %den.3, f32[3,1,32,1024]{3,2,1,0:T(8,128)} %vel.3, f32[1,32,1024]{2,1,0:T(8,128)} %prs.3, s32[1,32]{1,0:T(1,128)} %offx.1), custom_call_target="tpu_custom_call" | custom-call | tf_op jit(solution)/shard_map/pallas_call | solution.py:278
  2.5 14.6 %all-to-all-start = ((f32[256,1,128]{2,1,0:T(1,128)}), f32[256,1,128]{2,1,0:T(1,128)S(1)}, u32[]{:S(2)}, u32[]{:S(2)}) async-start(f32[256,1,128]{2,1,0:T(1,128)} %bitcast.5), calls=%async_computation | async-start | bytes 262144 | tf_op jit(solution)/shard_map/all_to_all | solution.py:285
  17.2 0.2 collective-permute-start
  17.4 5.8 %collective-permute-start.1 = (f32[5,8,1024]{2,1,0:T(8,128)}, f32[5,8,1024]{2,1,0:T(8,128)S(1)}, u32[]{:S(2)}, u32[]{:S(2)}) collective-permute-start(f32[5,8,1024]{2,1,0:T(8,128)} %get-tuple-element.7), channel_id=1, source_target_pairs={{0,248},{8,0},{16,8},{24,16},{32,24},{40,32},{48,40},{56,48},{64,5... | collective-permute-start | bytes 491528 | tf_op jit(solution)/shard_map/ppermute | solution.py:287
  23.2 5.1 %collective-permute-done.before = f32[5,8,1024]{2,1,0:T(8,128)S(1)} collective-permute-done((f32[5,8,1024]{2,1,0:T(8,128)}, f32[5,8,1024]{2,1,0:T(8,128)S(1)}, u32[]{:S(2)}, u32[]{:S(2)}) %collective-permute-start) | collective-permute-done | bytes 163872 | tf_op jit(solution)/shard_map/ppermute | solution.py:286
  28.3 0.0 copy-start.1
  28.3 0.0 collective-permute-done.1.after
  28.3 0.7 %copy-done.1 = f32[5,8,1024]{2,1,0:T(8,128)} copy-done((f32[5,8,1024]{2,1,0:T(8,128)}, f32[5,8,1024]{2,1,0:T(8,128)S(1)}, u32[]{:S(2)}) %copy-start.1) | copy-done | bytes 163864
  29.0 0.0 copy-start.2
  29.0 0.7 %copy-done.2 = f32[5,8,1024]{2,1,0:T(8,128)} copy-done((f32[5,8,1024]{2,1,0:T(8,128)}, f32[5,8,1024]{2,1,0:T(8,128)S(1)}, u32[]{:S(2)}) %copy-start.2) | copy-done | bytes 163864
  29.6 4.3 %shard_map.77.refs_0_ = f32[9,48,1024]{2,1,0:T(8,128)} custom-call(f32[1,32,1024]{2,1,0:T(8,128)} %den.3, f32[3,1,32,1024]{3,2,1,0:T(8,128)} %vel.3, f32[1,32,1024]{2,1,0:T(8,128)} %prs.3, f32[5,8,1024]{2,1,0:T(8,128)} %copy-done.1, f32[5,8,1024]{2,1,0:T(8,128)} %copy-done.2), custom_call_target="tpu_custom_call" | custom-call | flops 9830400 | bytes 3145728 | tf_op jit(solution)/shard_map/pallas_call | solution.py:289
  33.9 0.0 all-to-all-done
  33.9 0.0 copy-start
  33.9 0.6 %copy-done = f32[256,1,128]{2,1,0:T(1,128)} copy-done((f32[256,1,128]{2,1,0:T(1,128)}, f32[256,1,128]{2,1,0:T(1,128)S(1)}, u32[]{:S(2)}) %copy-start) | copy-done | bytes 131096
  34.6 7.9 %shard_map.78 = (f32[1,32,1024]{2,1,0:T(8,128)}, f32[3,1,32,1024]{3,2,1,0:T(8,128)}, f32[1,32,1024]{2,1,0:T(8,128)}) custom-call(f32[9,48,1024]{2,1,0:T(8,128)} %shard_map.77.refs_0_, f32[256,128]{1,0:T(8,128)} %bitcast.4, s32[1,1024]{1,0:T(1,128)} %refs_2_.1), custom_call_target="tpu_custom_call" | custom-call | tf_op jit(solution)/shard_map/pallas_call | solution.py:300
Async XLA Ops:
  2.5 31.4 %all-to-all-start = ((f32[256,1,128]{2,1,0:T(1,128)}), f32[256,1,128]{2,1,0:T(1,128)S(1)}, u32[]{:S(2)}, u32[]{:S(2)}) async-start(f32[256,1,128]{2,1,0:T(1,128)} %bitcast.5), calls=%async_computation | async-start | bytes 262144 | tf_op jit(solution)/shard_map/all_to_all | solution.py:285
  17.2 11.2 %collective-permute-start = (f32[5,8,1024]{2,1,0:T(8,128)}, f32[5,8,1024]{2,1,0:T(8,128)S(1)}, u32[]{:S(2)}, u32[]{:S(2)}) collective-permute-start(f32[5,8,1024]{2,1,0:T(8,128)} %get-tuple-element.6), channel_id=1, source_target_pairs={{0,8},{8,16},{16,24},{24,32},{32,40},{40,48},{48,56},{56,64},{64,7... | collective-permute-start | bytes 491528 | tf_op jit(solution)/shard_map/ppermute | solution.py:286
  17.4 10.9 %collective-permute-start.1 = (f32[5,8,1024]{2,1,0:T(8,128)}, f32[5,8,1024]{2,1,0:T(8,128)S(1)}, u32[]{:S(2)}, u32[]{:S(2)}) collective-permute-start(f32[5,8,1024]{2,1,0:T(8,128)} %get-tuple-element.7), channel_id=1, source_target_pairs={{0,248},{8,0},{16,8},{24,16},{32,24},{40,32},{48,40},{56,48},{64,5... | collective-permute-start | bytes 491528 | tf_op jit(solution)/shard_map/ppermute | solution.py:287
  28.3 0.7 %copy-start.1 = (f32[5,8,1024]{2,1,0:T(8,128)}, f32[5,8,1024]{2,1,0:T(8,128)S(1)}, u32[]{:S(2)}) copy-start(f32[5,8,1024]{2,1,0:T(8,128)S(1)} %collective-permute-done.before) | copy-start | bytes 491524
  29.0 0.7 %copy-start.2 = (f32[5,8,1024]{2,1,0:T(8,128)}, f32[5,8,1024]{2,1,0:T(8,128)S(1)}, u32[]{:S(2)}) copy-start(f32[5,8,1024]{2,1,0:T(8,128)S(1)} %collective-permute-done.1.after) | copy-start | bytes 491524
  33.9 0.7 %copy-start = (f32[256,1,128]{2,1,0:T(1,128)}, f32[256,1,128]{2,1,0:T(1,128)S(1)}, u32[]{:S(2)}) copy-start(f32[256,1,128]{2,1,0:T(1,128)S(1)} %all-to-all-done) | copy-start | bytes 393220
where the time goes:
time: 42.6 us; the launch traced here: 42.4 us
  starting transfers between devices  20.7 us (49%)
  Pallas kernels  14.1 us (33%)
  waiting for transfers between devices  5.09 us (12%)
  local copies, waits for them, and re-layouts  1.98 us (5%)
  between operations  0.64 us (2%)
    all_to_all x1, starting transfers between devices, body(): lax.all_to_all(pay, ('rows', 'cols'), split_axis=0, concat_axis=0, tiled=...  14.6 us
    pallas_call x1, Pallas kernels, body(): pl.pallas_call(lambda *refs: sweep_kernel(n_dev, n_cols, *refs), out_shap...  7.86 us
    ppermute x1, starting transfers between devices, body(): lax.ppermute(down, 'rows', [(i, (i - 1) % n_dev) for i in range(n_dev)])  5.84 us
    ppermute x1, waiting for transfers between devices, body(): lax.ppermute(up, 'rows', [(i, (i + 1) % n_dev) for i in range(n_dev)])  5.08 us
    pallas_call x1, Pallas kernels, body(): pl.pallas_call(face_kernel, out_shape=jax.ShapeDtypeStruct((9, total, n_x...  4.27 us
    unnamed x6, local copies, waits for them, and re-layouts  1.98 us
    pallas_call x1, Pallas kernels, body(): pl.pallas_call(speed_kernel, out_shape=(jax.ShapeDtypeStruct((everyone, L...  1.92 us
  transfers between devices with their start and end apart: 3, of which 1 were waited for; matrix products, arithmetic and copies ran while one was open for 0% of the time, Pallas kernels for 10%

commit v1 on v0

v1 whole, which is shorter than its diff:
```python
import jax
import jax.numpy as jnp
from jax import lax
from jax.experimental import pallas as pl
from jax.experimental.pallas import tpu as pltpu
from jax.sharding import PartitionSpec as P

SHIFT = 2
PAIR = 16
REACH = 3
A_LIMIT = 60 * 2**20
OWN_COST = 10**6
HALO_COST = 10**6
HALO = 8
LANES = 128
SUB = 8

courant = 0.4
adiabatic = 5.0 / 3.0


def inverse(v):
    return 1.0 / v


def clamp(v, a, b):
    return jnp.minimum(jnp.maximum(v, jnp.minimum(a, b)), jnp.maximum(a, b))


def face_of(am, a0, a1, a2):
    face = 7.0 / 12.0 * (a0 + a1) - 1.0 / 12.0 * (am + a2)
    return clamp(face, a0, a1)


def edges_of(a, face_before, face):
    triple = 3.0 * a
    low = clamp(face_before, a, triple - 2.0 * face)
    high = clamp(face, a, triple - 2.0 * face_before)
    return low, high


def sound_impedance(rho, inv_rho, p):
    return rho * jnp.sqrt(adiabatic * p * inv_rho)


def riemann(z, zn, u_right, u_left, p_right, p_left):
    inv = inverse(z + zn)
    us = (z * u_right + zn * u_left + p_right - p_left) * inv
    ps = (zn * p_right + z * p_left + z * zn * (u_right - u_left)) * inv
    return us, ps


def total_energy(inv_rho, p, un, ta, tb):
    return p * inv_rho * (1.0 / (adiabatic - 1.0)) + 0.5 * (un * un + ta * ta + tb * tb)


def flux_weights(d, f):
    rest = 1.0 - f
    df = d * f
    return d * rest * rest, df * (3.0 - 2.0 * f), df * rest


def primitive(mass, mn, ma, mb, energy):
    inv = inverse(mass)
    kinetic = 0.5 * (mn * mn + ma * ma + mb * mb) * inv
    return mass, mn * inv, ma * inv, mb * inv, (adiabatic - 1.0) * (energy - kinetic)


def split(v):
    return [v[:, k : k + LANES] for k in range(0, v.shape[1], LANES)]


def to_columns(halves, room):
    rows = [half[:, k : k + LANES] for k in range(0, halves[0].shape[1], LANES) for half in halves]
    room[...] = jnp.transpose(jnp.concatenate(rows, axis=0))
    return [room[pl.ds(j, SUB, stride=LANES // SUB), :] for j in range(LANES // SUB)]


def wrapped(tile, way):
    sub = lax.broadcasted_iota(jnp.int32, tile.shape, 0)
    turned = pltpu.roll(tile, way % SUB, 0)
    edge = 0 if way > 0 else SUB - 1
    return jnp.where(sub == edge, pltpu.roll(turned, way * PAIR % LANES, 1), turned)


def roll_x(v, k):
    parts = split(v)
    n = len(parts)
    moved = []
    for j in range(n):
        turns, source = divmod(j - k, n)
        moved.append(parts[source] if turns == 0 else wrapped(parts[source], -turns))
    return jnp.concatenate(moved, axis=1)


def profile_x(a):
    nxt = roll_x(a, -1)
    face = face_of(roll_x(a, 1), a, nxt, roll_x(a, -2))
    low, high = edges_of(a, roll_x(face, 1), face)
    return nxt, low, high


def lines_of(offx, first):
    shape = (SUB, LANES)
    lane = lax.broadcasted_iota(jnp.int32, shape, 1)
    row = lax.broadcasted_iota(jnp.int32, shape, 0)
    found = jnp.where(lane == row + first, jnp.broadcast_to(offx, shape), 0.0)
    return jnp.broadcast_to(jnp.sum(found, axis=1, keepdims=True), shape)


def speed_kernel(den, vel, prs, offx_hbm, pay, up, down, block, offx, line, sems, pack_sems):
    n_rows, n_x = den.shape[1:]
    off_load = pltpu.make_async_copy(offx_hbm, offx, sems.at[5])
    sources = (den.at[0], vel.at[0, 0], vel.at[1, 0], vel.at[2, 0], prs.at[0])
    loads = [pltpu.make_async_copy(sources[f], block.at[:, pl.ds(f * n_x, n_x)], sems.at[f]) for f in range(5)]
    for load in (*loads, off_load):
        load.start()
    line[...] = jnp.zeros_like(line)
    off_load.wait()
    line[:, 0:n_rows] = offx[...].astype(jnp.float32)
    for first in (0, n_rows - HALO):
        block[first : first + HALO, 5 * n_x :] = lines_of(line[...], first)
    for load in loads:
        load.wait()
    packs = [
        pltpu.make_async_copy(block.at[pl.ds(first, HALO), :], out, pack_sems.at[k])
        for k, (out, first) in enumerate(((up, n_rows - HALO), (down, 0)))
    ]
    for pack in packs:
        pack.start()
    peak = None
    for g in range(n_rows // SUB):
        rho, un, ta, p = (block[g * SUB : (g + 1) * SUB, f * n_x : (f + 1) * n_x] for f in (0, 1, 2, 4))
        s = jnp.maximum(jnp.abs(un), jnp.abs(ta)) + jnp.sqrt(adiabatic * p / rho)
        peak = s if peak is None else jnp.maximum(peak, s)
    tiles = split(peak)
    while len(tiles) > 1:
        tiles = [jnp.maximum(x, y) for x, y in zip(tiles[::2], tiles[1::2])]
    pay[...] = jnp.broadcast_to(jnp.max(tiles[0], axis=0, keepdims=True), pay.shape)
    for pack in packs:
        pack.wait()


def prepare(halves, state, row, by, rooms):
    rho, un, ta, tb, p = (
        jnp.concatenate(to_columns([h[f] for h in halves], rooms.at[f]), axis=1) for f in range(5)
    )
    lines = jnp.concatenate([h[5] for h in halves] * (LANES // PAIR), axis=0)
    by[pl.ds(row, SUB), :] = jnp.transpose(lines)[0:SUB, :]
    inv = inverse(rho)
    z = sound_impedance(rho, inv, p)
    _, u_low, u_high = profile_x(un)
    _, p_low, p_high = profile_x(p)
    us, ps = riemann(z, roll_x(z, -1), u_high, roll_x(u_low, -1), p_high, roll_x(p_low, -1))
    work = us * ps
    o = pl.ds(row, SUB)
    values = (
        rho, us, us - roll_x(us, 1), un, (ps - roll_x(ps, 1)) * inv, ta, tb,
        total_energy(inv, p, un, ta, tb), (work - roll_x(work, 1)) * inv,
    )
    for n, v in enumerate(values):
        tiles = split(v)
        ends = [wrapped(t, 1) for t in tiles[-REACH:]], [wrapped(t, -1) for t in tiles[:REACH]]
        for t, tile in enumerate(ends[0] + tiles + ends[1]):
            state[n, o, t * LANES : (t + 1) * LANES] = tile


def own_kernel(den, vel, prs, offx, offy, state, rows_by, lines_by, line, rooms):
    n_rows, n_x = den.shape[1:]
    for k in range(n_x // LANES):
        lines_by[k : k + 1, :] = offy[:, k * LANES : (k + 1) * LANES].astype(jnp.float32)
    line[...] = jnp.zeros_like(line)
    line[:, 0:n_rows] = offx[...].astype(jnp.float32)
    for g in range(n_rows // PAIR):
        halves = []
        for first in range(g * PAIR, (g + 1) * PAIR, SUB):
            r = pl.ds(first, SUB)
            halves.append(
                [den[0, r, :], vel[0, 0, r, :], vel[1, 0, r, :], vel[2, 0, r, :], prs[0, r, :], lines_of(line[...], first)]
            )
        prepare(halves, state, g * SUB, rows_by, rooms.at[g])


def halo_kernel(before, after, state, rows_by, rooms):
    n_x = (before.shape[1] - LANES) // 5
    halves = [[ref[:, f * n_x : (f + 1) * n_x] for f in range(5)] + [ref[:, 5 * n_x :]] for ref in (before, after)]
    prepare(halves, state, 0, rows_by, rooms)


def sweep_kernel(
    state, halo_state, got, rows_by, halo_by, lines_by, den_out, vel_out, prs_out,
    columns, swept, rows_out, tiles_out, out_sem,
):
    n_rows, n_x = den_out.shape[1:]
    n_tiles = n_x // LANES
    groups = n_rows // SUB + 2
    n_steps = LANES // SUB
    top = [got[k * SUB : (k + 1) * SUB, :] for k in range(got.shape[0] // SUB)]
    while len(top) > 1:
        top = [jnp.maximum(x, y) for x, y in zip(top[::2], top[1::2])]
    dt = courant / jnp.max(jnp.max(top[0], axis=0, keepdims=True), axis=1, keepdims=True)

    def x_group(state, row, offsets, n, late):
        o = pl.ds(row, SUB)

        def tile_of(n, t):
            return state[n, o, (t + REACH) * LANES : (t + REACH + 1) * LANES]

        width, inv_w, amount, face, edges, flux, result = {}, {}, {}, {}, {}, {}, {}
        shifted = {k: offsets == k for k in range(-SHIFT, SHIFT + 1) if k}

        def put(j):
            for f in range(5):
                v = result[j][f]
                for k, mask in shifted.items():
                    v = jnp.where(mask, result[j - k][f], v)
                columns[n, f, pl.ds(j, SUB, stride=n_steps), :] = v

        for t in range(-REACH, n_steps + REACH):
            width[t] = 1.0 + dt * tile_of(2, t)
            inv_w[t] = inverse(width[t])
            lag = tile_of(0, t) * inv_w[t]
            amount[t] = (
                lag, lag * (tile_of(3, t) - dt * tile_of(4, t)), lag * tile_of(5, t), lag * tile_of(6, t),
                lag * (tile_of(7, t) - dt * tile_of(8, t)),
            )
            if late:
                late.pop(0)()
            i = t - 2
            if i >= -2:
                face[i] = [face_of(*(amount[i + k][f] for k in (-1, 0, 1, 2))) for f in range(5)]
            if i >= -1:
                edges[i] = [edges_of(amount[i][f], face[i - 1][f], face[i][f]) for f in range(5)]
            i = t - 3
            if i >= -1:
                us = tile_of(1, i)
                up = us > 0.0
                d = dt * us
                k1, k2, k3 = flux_weights(d, jnp.abs(d) * jnp.where(up, inv_w[i], inv_w[i + 1]))
                flux[i] = []
                for f in range(5):
                    (low, high), (low_n, high_n) = edges[i][f], edges[i + 1][f]
                    near = jnp.where(up, high, low_n)
                    far = jnp.where(up, low, high_n)
                    mean = jnp.where(up, amount[i][f], amount[i + 1][f])
                    flux[i].append(k1 * near + k2 * mean - k3 * far)
            if i >= 0:
                kept = [tile_of(0, i)] + [amount[i][f] * width[i] for f in range(1, 5)]
                result[i] = primitive(*(kept[f] + flux[i - 1][f] - flux[i][f] for f in range(5)))
                if i < SHIFT:
                    result[n_steps + i] = [wrapped(v, -1) for v in result[i]]
                if i >= n_steps - SHIFT:
                    result[i - n_steps] = [wrapped(v, 1) for v in result[i]]
                if i >= 2 * SHIFT:
                    put(i - SHIFT)
        for j in (n_steps - 2, n_steps - 1, 0, 1):
            late.append(lambda j=j: put(j))

    def turn(n, f, first, second):
        natural = jnp.transpose(columns[n, f])
        for k in range(n_tiles):
            for h, group in enumerate((first, second)):
                at = (k * 2 + h) * SUB
                swept[f, pl.ds((group * n_tiles + k) * SUB, SUB), :] = natural[at : at + SUB, :]

    n_own = n_rows // PAIR
    late, turns = [], []
    x_group(halo_state, 0, halo_by[...], 0, late)
    for g in range(n_own):
        x_group(state, g * SUB, rows_by[g * SUB : (g + 1) * SUB, :], g + 1, late)
        if g == 0:
            turns = [(0, f, 0, groups - 1) for f in range(5)]
        else:
            turns = [(g, f, 2 * g - 1, 2 * g) for f in range(5)]
        for args in turns:
            turn(*args)
    for put_late in late:
        put_late()
    turns = [(n_own, f, 2 * n_own - 1, 2 * n_own) for f in range(5)]

    total = groups * SUB

    def load_row(r):
        at = (r // SUB) * n_tiles * SUB + r % SUB
        rho, ta, un, tb, p = (swept[f, pl.ds(at, SUB, stride=SUB), :] for f in range(5))
        return rho, un, ta, tb, p

    oy = lines_by[...]
    moved = {k: oy == k for k in range(-SHIFT, SHIFT + 1) if k}
    cells, inv_rho, imp, faces, edges = {}, {}, {}, {}, {}
    stars, lags, weights, q_faces, q_edges, fluxes, done = {}, {}, {}, {}, {}, {}, {}
    copies, waiting = [], []
    targets = (den_out.at[0], vel_out.at[1, 0], vel_out.at[0, 0], vel_out.at[2, 0], prs_out.at[0])

    def turn_back(a, f):
        here = pl.ds(a * SUB, SUB)
        tiles = [rows_out[f, pl.ds((a * n_tiles + j) * SUB, SUB), :] for j in range(n_tiles)]
        for k, tile in enumerate(tiles):
            tiles_out[f, here, pl.ds(k * LANES, LANES)] = tile

    def send(a):
        here = pl.ds(a * SUB, SUB)
        for f in range(5):
            copies.append(
                pltpu.make_async_copy(tiles_out.at[f, here, :], targets[f].at[here, :], out_sem.at[f, a])
            )
            copies[-1].start()

    for r in range(total):
        if turns:
            turn(*turns.pop(0))
        cells[r] = load_row(r)
        rho, un, ta, tb, p = cells[r]
        inv_rho[r] = inverse(rho)
        imp[r] = sound_impedance(rho, inv_rho[r], p)
        i = r - 2
        if i >= 1:
            faces[i] = [face_of(*(cells[i + k][f] for k in (-1, 0, 1, 2))) for f in (1, 4)]
        if i >= 2:
            edges[i] = [edges_of(cells[i][f], faces[i - 1][n], faces[i][n]) for n, f in enumerate((1, 4))]
        i = r - 3
        if i >= 2:
            (_, u_right), (_, p_right) = edges[i]
            (u_left, _), (p_left, _) = edges[i + 1]
            us, ps = riemann(imp[i], imp[i + 1], u_right, u_left, p_right, p_left)
            stars[i] = us, ps, us * ps, dt * us
        if i >= 3:
            rho, un, ta, tb, p = cells[i]
            us, ps, work, d = stars[i]
            _, ps_b, work_b, d_b = stars[i - 1]
            w = 1.0 + d - d_b
            inv_w = inverse(w)
            rate = dt * inv_rho[i]
            lag = rho * inv_w
            e = total_energy(inv_rho[i], p, un, ta, tb)
            lags[i] = (
                lag, lag * (un - rate * (ps - ps_b)), lag * ta, lag * tb, lag * (e - rate * (work - work_b)),
            )
            weights[i] = w, inv_w
        i = r - 5
        if i >= 4:
            q_faces[i] = [face_of(*(lags[i + k][f] for k in (-1, 0, 1, 2))) for f in range(5)]
        if i >= 5:
            q_edges[i] = [edges_of(lags[i][f], q_faces[i - 1][f], q_faces[i][f]) for f in range(5)]
        i = r - 6
        if i >= 5:
            d = stars[i][3]
            up = d > 0.0
            f_up = jnp.abs(d) * jnp.where(up, weights[i][1], weights[i + 1][1])
            k1, k2, k3 = flux_weights(d, f_up)
            fluxes[i] = []
            for f in range(5):
                low, high = q_edges[i][f]
                low_n, high_n = q_edges[i + 1][f]
                near = jnp.where(up, high, low_n)
                far = jnp.where(up, low, high_n)
                fluxes[i].append(k1 * near + k2 * jnp.where(up, lags[i][f], lags[i + 1][f]) - k3 * far)
        if i >= 6:
            done[i] = primitive(
                *(lags[i][f] * weights[i][0] + fluxes[i - 1][f] - fluxes[i][f] for f in range(5))
            )
        i = r - 8
        if i >= HALO:
            j = i - HALO
            a, b = divmod(j, SUB)
            for f in range(5):
                v = done[i][f]
                for k, mask in moved.items():
                    v = jnp.where(mask, done[i - k][f], v)
                rows_out[f, pl.ds(a * n_tiles * SUB + b, SUB, stride=SUB), :] = v
            if b == SUB - 1:
                if a:
                    send(a - 1)
                waiting += [(a, f) for f in range(5)]
        if waiting:
            turn_back(*waiting.pop(0))
    for a, f in waiting:
        turn_back(a, f)
    send(n_rows // SUB - 1)
    for copy in copies:
        copy.wait()


def body(n_dev, n_cols, density, velocity, pressure, offsets_x, offsets_y):
    n_rows, n_x = density.shape[1:]
    f32 = jnp.float32
    vmem = pl.BlockSpec(memory_space=pltpu.VMEM)
    everyone = n_dev * n_cols
    small = pltpu.CompilerParams(vmem_limit_bytes=16 * 2**20)
    hbm = pl.BlockSpec(memory_space=pltpu.HBM)
    wide = 5 * n_x + LANES
    halo = jax.ShapeDtypeStruct((HALO, wide), f32)
    pay, up, down = pl.pallas_call(
        speed_kernel,
        out_shape=(jax.ShapeDtypeStruct((everyone, LANES), f32), halo, halo),
        in_specs=[hbm] * 4,
        out_specs=[vmem] + [hbm] * 2,
        scratch_shapes=[
            pltpu.VMEM((n_rows, wide), f32),
            pltpu.VMEM(offsets_x.shape, jnp.int32),
            pltpu.VMEM((1, LANES), f32),
            pltpu.SemaphoreType.DMA((6,)),
            pltpu.SemaphoreType.DMA((2,)),
        ],
        compiler_params=pltpu.CompilerParams(vmem_limit_bytes=A_LIMIT),
    )(density, velocity, pressure, offsets_x)
    got = lax.all_to_all(pay, ("rows", "cols"), split_axis=0, concat_axis=0, tiled=True)
    before = lax.ppermute(up, "rows", [(i, (i + 1) % n_dev) for i in range(n_dev)])
    after = lax.ppermute(down, "rows", [(i, (i - 1) % n_dev) for i in range(n_dev)])
    long = (LANES // SUB + 2 * REACH) * LANES
    rooms = pltpu.VMEM((5, LANES, LANES), f32)
    n_own = n_rows // PAIR
    state, rows_by, lines_by = pl.pallas_call(
        own_kernel,
        out_shape=(
            jax.ShapeDtypeStruct((9, n_own * SUB, long), f32),
            jax.ShapeDtypeStruct((n_own * SUB, LANES), f32),
            jax.ShapeDtypeStruct((SUB, LANES), f32),
        ),
        in_specs=[vmem] * 5,
        out_specs=[vmem] * 3,
        scratch_shapes=[pltpu.VMEM((1, LANES), f32), pltpu.VMEM((n_own, 5, LANES, LANES), f32)],
        compiler_params=small,
        cost_estimate=pl.CostEstimate(flops=OWN_COST, bytes_accessed=10**6, transcendentals=0),
    )(density, velocity, pressure, offsets_x, offsets_y)
    halo_state, halo_by = pl.pallas_call(
        halo_kernel,
        out_shape=(
            jax.ShapeDtypeStruct((9, SUB, long), f32), jax.ShapeDtypeStruct((SUB, LANES), f32),
        ),
        in_specs=[vmem] * 2,
        out_specs=[vmem] * 2,
        scratch_shapes=[rooms],
        compiler_params=small,
        cost_estimate=pl.CostEstimate(flops=HALO_COST, bytes_accessed=10**6, transcendentals=0),
    )(before, after)
    plane = jax.ShapeDtypeStruct(density.shape, f32)
    tall = (n_rows + 2 * HALO) * n_x // LANES
    short = n_rows * n_x // LANES
    return pl.pallas_call(
        sweep_kernel,
        out_shape=(plane, jax.ShapeDtypeStruct(velocity.shape, f32), plane),
        in_specs=[vmem] * 6,
        out_specs=[hbm] * 3,
        scratch_shapes=[
            pltpu.VMEM((n_own + 1, 5, LANES, LANES), f32),
            pltpu.VMEM((5, tall, LANES), f32),
            pltpu.VMEM((5, short, LANES), f32),
            pltpu.VMEM((5, n_rows, n_x), f32),
            pltpu.SemaphoreType.DMA((5, n_rows // SUB)),
        ],
        compiler_params=small,
    )(state, halo_state, got, rows_by, halo_by, lines_by)


def solution(mesh):
    n_dev, n_cols = mesh.shape["rows"], mesh.shape["cols"]
    return jax.shard_map(
        lambda *arrays: body(n_dev, n_cols, *arrays),
        mesh=mesh,
        in_specs=(
            P("cols", "rows", None),
            P(None, "cols", "rows", None),
            P("cols", "rows", None),
            P("cols", "rows"),
            P("cols", None),
        ),
        out_specs=(P("cols", "rows", None), P(None, "cols", "rows", None), P("cols", "rows", None)),
        check_vma=False,
    )
```

time: 42.6 us -> 37 us (0.87)
  the two profiles are of different devices: /device:TPU:8 before, /device:TPU:1 now
where the time goes in v1:
time: 37 us; the launch traced here: 36.7 us
  starting transfers between devices  18 us (49%)
  Pallas kernels  8.85 us (24%)
  waiting for transfers between devices  5.06 us (14%)
  local copies, waits for them, and re-layouts  4.14 us (11%)
  between operations  0.67 us (2%)
    all_to_all x1, starting transfers between devices, body(): lax.all_to_all(pay, ('rows', 'cols'), split_axis=0, concat_axis=0, tiled=...  15.7 us
    pallas_call x1, Pallas kernels, body(): pl.pallas_call(sweep_kernel, out_shape=(plane, jax.ShapeDtypeStruct(veloc...  4.76 us
    all_to_all x1, waiting for transfers between devices, body(): lax.all_to_all(pay, ('rows', 'cols'), split_axis=0, concat_axis=0, tiled=...  4.4 us
    unnamed x10, local copies, waits for them, and re-layouts  4.14 us
    pallas_call x1, Pallas kernels, body(): pl.pallas_call(speed_kernel, out_shape=(jax.ShapeDtypeStruct((everyone, L...  2.6 us
    ppermute x1, starting transfers between devices, body(): lax.ppermute(up, 'rows', [(i, (i + 1) % n_dev) for i in range(n_dev)])  1.83 us
    pallas_call x1, Pallas kernels, body(): pl.pallas_call(own_kernel, out_shape=(jax.ShapeDtypeStruct((9, n_own * SU...  0.94 us
  transfers between devices with their start and end apart: 3, of which 2 were waited for; matrix products, arithmetic and copies ran while one was open for 0% of the time, Pallas kernels for 4%

profile of v1, /device:TPU:1, one launch (start us, length us, event | category | flops | bytes accessed | tf_op | source)
XLA Modules:
  0.0 36.7 jit_solution(3662530247466011579)
XLA Ops:
  0.6 2.6 %shard_map.77 = (f32[256,128]{1,0:T(8,128)}, f32[8,5248]{1,0:T(8,128)}, f32[8,5248]{1,0:T(8,128)}) custom-call(f32[1,32,1024]{2,1,0:T(8,128)} %den.3, f32[3,1,32,1024]{3,2,1,0:T(8,128)} %vel.3, f32[1,32,1024]{2,1,0:T(8,128)} %prs.3, s32[1,32]{1,0:T(1,128)} %offx_hbm.1), custom_call_target="tpu_custom_call" | custom-call | tf_op jit(solution)/shard_map/pallas_call | solution.py:393
  3.2 15.7 %all-to-all-start = ((f32[256,1,128]{2,1,0:T(1,128)}), f32[256,1,128]{2,1,0:T(1,128)S(1)}, u32[]{:S(2)}, u32[]{:S(2)}) async-start(f32[256,1,128]{2,1,0:T(1,128)} %bitcast.5), calls=%async_computation | async-start | bytes 262144 | tf_op jit(solution)/shard_map/all_to_all | solution.py:407
  18.9 1.8 %collective-permute-start = (f32[8,5248]{1,0:T(8,128)}, f32[8,5248]{1,0:T(8,128)S(1)}, u32[]{:S(2)}, u32[]{:S(2)}) collective-permute-start(f32[8,5248]{1,0:T(8,128)} %get-tuple-element.12), channel_id=1, source_target_pairs={{0,8},{8,16},{16,24},{24,32},{32,40},{40,48},{48,56},{56,64},{64,7... | collective-permute-start | bytes 503816 | tf_op jit(solution)/shard_map/ppermute | solution.py:408
  20.7 0.5 %collective-permute-start.1 = (f32[8,5248]{1,0:T(8,128)}, f32[8,5248]{1,0:T(8,128)S(1)}, u32[]{:S(2)}, u32[]{:S(2)}) collective-permute-start(f32[8,5248]{1,0:T(8,128)} %get-tuple-element.13), channel_id=1, source_target_pairs={{0,248},{8,0},{16,8},{24,16},{32,24},{40,32},{48,40},{56,48},{64,5... | collective-permute-start | bytes 503816 | tf_op jit(solution)/shard_map/ppermute | solution.py:409
  21.2 0.0 copy-start
  21.2 1.0 %copy-done = f32[3,1,32,1024]{3,2,1,0:T(8,128)S(1)} copy-done((f32[3,1,32,1024]{3,2,1,0:T(8,128)S(1)}, f32[3,1,32,1024]{3,2,1,0:T(8,128)}, u32[]{:S(2)}) %copy-start) | copy-done | bytes 393240
  22.2 0.0 copy-start.1
  22.2 0.9 %copy-done.1 = f32[1,32,1024]{2,1,0:T(8,128)S(1)} copy-done((f32[1,32,1024]{2,1,0:T(8,128)S(1)}, f32[1,32,1024]{2,1,0:T(8,128)}, u32[]{:S(2)}) %copy-start.1) | copy-done | bytes 131096
  23.1 0.0 copy-start.2
  23.1 0.9 %copy-done.2 = f32[1,32,1024]{2,1,0:T(8,128)S(1)} copy-done((f32[1,32,1024]{2,1,0:T(8,128)S(1)}, f32[1,32,1024]{2,1,0:T(8,128)}, u32[]{:S(2)}) %copy-start.2) | copy-done | bytes 131096
  24.0 0.0 copy-start.3
  24.0 0.7 %copy-done.3 = s32[1,1024]{1,0:T(1,128)S(1)} copy-done((s32[1,1024]{1,0:T(1,128)S(1)}, s32[1,1024]{1,0:T(1,128)}, u32[]{:S(2)}) %copy-start.3) | copy-done | bytes 4120
  24.7 0.0 copy-start.4
  24.7 0.7 %copy-done.4 = s32[1,32]{1,0:T(1,128)S(1)} copy-done((s32[1,32]{1,0:T(1,128)S(1)}, s32[1,32]{1,0:T(1,128)}, u32[]{:S(2)}) %copy-start.4) | copy-done | bytes 152
  25.4 0.9 %shard_map.76 = (f32[9,16,2816]{2,1,0:T(8,128)S(1)}, f32[16,128]{1,0:T(8,128)S(1)}, f32[8,128]{1,0:T(8,128)S(1)}) custom-call(f32[1,32,1024]{2,1,0:T(8,128)S(1)} %copy-done.1, f32[3,1,32,1024]{3,2,1,0:T(8,128)S(1)} %copy-done, f32[1,32,1024]{2,1,0:T(8,128)S(1)} %copy-done.2, s32[1,32]{1,0:T(1,128)S(1)} %copy-done.4, s32[1,1024]{1,0:T(1,128)S(1)} %copy-done.3), custom_call_target="tpu_custom_call" | custom-call | flops 1000000 | bytes 1000000 | tf_op jit(solution)/shard_map/pallas_call | solution.py:413
  26.3 0.0 collective-permute-done.before
  26.3 0.7 %collective-permute-done.1.after = f32[8,5248]{1,0:T(8,128)S(1)} collective-permute-done((f32[8,5248]{1,0:T(8,128)}, f32[8,5248]{1,0:T(8,128)S(1)}, u32[]{:S(2)}, u32[]{:S(2)}) %collective-permute-start.1) | collective-permute-done | bytes 167968 | tf_op jit(solution)/shard_map/ppermute | solution.py:409
  27.0 0.5 %shard_map.78 = (f32[9,8,2816]{2,1,0:T(8,128)S(1)}, f32[8,128]{1,0:T(8,128)S(1)}) custom-call(f32[8,5248]{1,0:T(8,128)S(1)} %collective-permute-done.before, f32[8,5248]{1,0:T(8,128)S(1)} %collective-permute-done.1.after), custom_call_target="tpu_custom_call" | custom-call | flops 1000000 | bytes 1000000 | tf_op jit(solution)/shard_map/pallas_call | solution.py:426
  27.5 4.4 %all-to-all-done = f32[256,1,128]{2,1,0:T(1,128)S(1)} async-done(((f32[256,1,128]{2,1,0:T(1,128)}), f32[256,1,128]{2,1,0:T(1,128)S(1)}, u32[]{:S(2)}, u32[]{:S(2)}) %all-to-all-start) | async-done | bytes 131104 | tf_op jit(solution)/shard_map/all_to_all | solution.py:407
  31.9 4.8 %shard_map.79 = (f32[1,32,1024]{2,1,0:T(8,128)}, f32[3,1,32,1024]{3,2,1,0:T(8,128)}, f32[1,32,1024]{2,1,0:T(8,128)}) custom-call(f32[9,16,2816]{2,1,0:T(8,128)S(1)} %get-tuple-element.11.state, f32[9,8,2816]{2,1,0:T(8,128)S(1)} %get-tuple-element.14.halo_state, f32[256,128]{1,0:T(8,128)S(1)} %bitcast.4, f32[16,128]{1,0:T(8,128)S(1)} %get-tuple-element.16.rows_by, ...), custom_call_target="tpu_custom_call" | custom-call | tf_op jit(solution)/shard_map/pallas_call | solution.py:440
Async XLA Ops:
  3.2 28.7 %all-to-all-start = ((f32[256,1,128]{2,1,0:T(1,128)}), f32[256,1,128]{2,1,0:T(1,128)S(1)}, u32[]{:S(2)}, u32[]{:S(2)}) async-start(f32[256,1,128]{2,1,0:T(1,128)} %bitcast.5), calls=%async_computation | async-start | bytes 262144 | tf_op jit(solution)/shard_map/all_to_all | solution.py:407
  18.9 7.4 %collective-permute-start = (f32[8,5248]{1,0:T(8,128)}, f32[8,5248]{1,0:T(8,128)S(1)}, u32[]{:S(2)}, u32[]{:S(2)}) collective-permute-start(f32[8,5248]{1,0:T(8,128)} %get-tuple-element.12), channel_id=1, source_target_pairs={{0,8},{8,16},{16,24},{24,32},{32,40},{40,48},{48,56},{56,64},{64,7... | collective-permute-start | bytes 503816 | tf_op jit(solution)/shard_map/ppermute | solution.py:408
  20.7 6.2 %collective-permute-start.1 = (f32[8,5248]{1,0:T(8,128)}, f32[8,5248]{1,0:T(8,128)S(1)}, u32[]{:S(2)}, u32[]{:S(2)}) collective-permute-start(f32[8,5248]{1,0:T(8,128)} %get-tuple-element.13), channel_id=1, source_target_pairs={{0,248},{8,0},{16,8},{24,16},{32,24},{40,32},{48,40},{56,48},{64,5... | collective-permute-start | bytes 503816 | tf_op jit(solution)/shard_map/ppermute | solution.py:409
  21.2 1.0 %copy-start = (f32[3,1,32,1024]{3,2,1,0:T(8,128)S(1)}, f32[3,1,32,1024]{3,2,1,0:T(8,128)}, u32[]{:S(2)}) copy-start(f32[3,1,32,1024]{3,2,1,0:T(8,128)} %vel.3) | copy-start | bytes 1179652
  22.2 0.9 %copy-start.1 = (f32[1,32,1024]{2,1,0:T(8,128)S(1)}, f32[1,32,1024]{2,1,0:T(8,128)}, u32[]{:S(2)}) copy-start(f32[1,32,1024]{2,1,0:T(8,128)} %den.3) | copy-start | bytes 393220
  23.1 0.9 %copy-start.2 = (f32[1,32,1024]{2,1,0:T(8,128)S(1)}, f32[1,32,1024]{2,1,0:T(8,128)}, u32[]{:S(2)}) copy-start(f32[1,32,1024]{2,1,0:T(8,128)} %prs.3) | copy-start | bytes 393220
  24.0 0.7 %copy-start.3 = (s32[1,1024]{1,0:T(1,128)S(1)}, s32[1,1024]{1,0:T(1,128)}, u32[]{:S(2)}) copy-start(s32[1,1024]{1,0:T(1,128)} %offy.1) | copy-start | bytes 12292
  24.7 0.7 %copy-start.4 = (s32[1,32]{1,0:T(1,128)S(1)}, s32[1,32]{1,0:T(1,128)}, u32[]{:S(2)}) copy-start(s32[1,32]{1,0:T(1,128)} %offx_hbm.1) | copy-start | bytes 388

commit v2 on v1

--- a/solution.py
+++ b/solution.py
@@ -11,6 +11,7 @@
 A_LIMIT = 60 * 2**20
 OWN_COST = 10**6
 HALO_COST = 10**6
+LEAD = 16
 HALO = 8
 LANES = 128
 SUB = 8
@@ -108,7 +109,7 @@
     return jnp.broadcast_to(jnp.sum(found, axis=1, keepdims=True), shape)
 
 
-def speed_kernel(den, vel, prs, offx_hbm, pay, up, down, block, offx, line, sems, pack_sems):
+def speed_kernel(den, vel, prs, offx_hbm, pay_hbm, up, down, pay, block, offx, line, sems, pack_sems):
     n_rows, n_x = den.shape[1:]
     off_load = pltpu.make_async_copy(offx_hbm, offx, sems.at[5])
     sources = (den.at[0], vel.at[0, 0], vel.at[1, 0], vel.at[2, 0], prs.at[0])
@@ -137,6 +138,8 @@
     while len(tiles) > 1:
         tiles = [jnp.maximum(x, y) for x, y in zip(tiles[::2], tiles[1::2])]
     pay[...] = jnp.broadcast_to(jnp.max(tiles[0], axis=0, keepdims=True), pay.shape)
+    packs.append(pltpu.make_async_copy(pay, pay_hbm, pack_sems.at[2]))
+    packs[-1].start()
     for pack in packs:
         pack.wait()
 
@@ -200,7 +203,7 @@
         top = [jnp.maximum(x, y) for x, y in zip(top[::2], top[1::2])]
     dt = courant / jnp.max(jnp.max(top[0], axis=0, keepdims=True), axis=1, keepdims=True)
 
-    def x_group(state, row, offsets, n, late):
+    def x_group(state, row, offsets, block, late):
         o = pl.ds(row, SUB)
 
         def tile_of(n, t):
@@ -214,7 +217,7 @@
                 v = result[j][f]
                 for k, mask in shifted.items():
                     v = jnp.where(mask, result[j - k][f], v)
-                columns[n, f, pl.ds(j, SUB, stride=n_steps), :] = v
+                columns[block, f, pl.ds(j, SUB, stride=n_steps), :] = v
 
         for t in range(-REACH, n_steps + REACH):
             width[t] = 1.0 + dt * tile_of(2, t)
@@ -227,23 +230,26 @@
             if late:
                 late.pop(0)()
             i = t - 2
-            if i >= -2:
-                face[i] = [face_of(*(amount[i + k][f] for k in (-1, 0, 1, 2))) for f in range(5)]
-            if i >= -1:
-                edges[i] = [edges_of(amount[i][f], face[i - 1][f], face[i][f]) for f in range(5)]
-            i = t - 3
-            if i >= -1:
-                us = tile_of(1, i)
+            n = t - 3
+            if n >= -1:
+                us = tile_of(1, n)
                 up = us > 0.0
                 d = dt * us
-                k1, k2, k3 = flux_weights(d, jnp.abs(d) * jnp.where(up, inv_w[i], inv_w[i + 1]))
-                flux[i] = []
-                for f in range(5):
-                    (low, high), (low_n, high_n) = edges[i][f], edges[i + 1][f]
+                k1, k2, k3 = flux_weights(d, jnp.abs(d) * jnp.where(up, inv_w[n], inv_w[n + 1]))
+                flux[n] = []
+            face[i], edges[i] = [], []
+            for f in range(5):
+                if i >= -2:
+                    face[i].append(face_of(*(amount[i + k][f] for k in (-1, 0, 1, 2))))
+                if i >= -1:
+                    edges[i].append(edges_of(amount[i][f], face[i - 1][f], face[i][f]))
+                if n >= -1:
+                    (low, high), (low_n, high_n) = edges[n][f], edges[n + 1][f]
                     near = jnp.where(up, high, low_n)
                     far = jnp.where(up, low, high_n)
-                    mean = jnp.where(up, amount[i][f], amount[i + 1][f])
-                    flux[i].append(k1 * near + k2 * mean - k3 * far)
+                    mean = jnp.where(up, amount[n][f], amount[n + 1][f])
+                    flux[n].append(k1 * near + k2 * mean - k3 * far)
+            i = n
             if i >= 0:
                 kept = [tile_of(0, i)] + [amount[i][f] * width[i] for f in range(1, 5)]
                 result[i] = primitive(*(kept[f] + flux[i - 1][f] - flux[i][f] for f in range(5)))
@@ -306,7 +312,7 @@
             )
             copies[-1].start()
 
-    for r in range(total):
+    def solve_row(r):
         if turns:
             turn(*turns.pop(0))
         cells[r] = load_row(r)
@@ -337,24 +343,27 @@
                 lag, lag * (un - rate * (ps - ps_b)), lag * ta, lag * tb, lag * (e - rate * (work - work_b)),
             )
             weights[i] = w, inv_w
+
+    def remap_row(r):
         i = r - 5
-        if i >= 4:
-            q_faces[i] = [face_of(*(lags[i + k][f] for k in (-1, 0, 1, 2))) for f in range(5)]
-        if i >= 5:
-            q_edges[i] = [edges_of(lags[i][f], q_faces[i - 1][f], q_faces[i][f]) for f in range(5)]
-        i = r - 6
-        if i >= 5:
-            d = stars[i][3]
+        n = r - 6
+        if n >= 5:
+            d = stars[n][3]
             up = d > 0.0
-            f_up = jnp.abs(d) * jnp.where(up, weights[i][1], weights[i + 1][1])
-            k1, k2, k3 = flux_weights(d, f_up)
-            fluxes[i] = []
-            for f in range(5):
-                low, high = q_edges[i][f]
-                low_n, high_n = q_edges[i + 1][f]
+            k1, k2, k3 = flux_weights(d, jnp.abs(d) * jnp.where(up, weights[n][1], weights[n + 1][1]))
+            fluxes[n] = []
+        q_faces[i], q_edges[i] = [], []
+        for f in range(5):
+            if i >= 4:
+                q_faces[i].append(face_of(*(lags[i + k][f] for k in (-1, 0, 1, 2))))
+            if i >= 5:
+                q_edges[i].append(edges_of(lags[i][f], q_faces[i - 1][f], q_faces[i][f]))
+            if n >= 5:
+                (low, high), (low_n, high_n) = q_edges[n][f], q_edges[n + 1][f]
                 near = jnp.where(up, high, low_n)
                 far = jnp.where(up, low, high_n)
-                fluxes[i].append(k1 * near + k2 * jnp.where(up, lags[i][f], lags[i + 1][f]) - k3 * far)
+                fluxes[n].append(k1 * near + k2 * jnp.where(up, lags[n][f], lags[n + 1][f]) - k3 * far)
+        i = n
         if i >= 6:
             done[i] = primitive(
                 *(lags[i][f] * weights[i][0] + fluxes[i - 1][f] - fluxes[i][f] for f in range(5))
@@ -371,9 +380,15 @@
             if b == SUB - 1:
                 if a:
                     send(a - 1)
-                waiting += [(a, f) for f in range(5)]
+                waiting.extend((a, f) for f in range(5))
         if waiting:
             turn_back(*waiting.pop(0))
+
+    for r in range(total + LEAD):
+        if r < total:
+            solve_row(r)
+        if r >= LEAD:
+            remap_row(r - LEAD)
     for a, f in waiting:
         turn_back(a, f)
     send(n_rows // SUB - 1)
@@ -394,13 +409,14 @@
         speed_kernel,
         out_shape=(jax.ShapeDtypeStruct((everyone, LANES), f32), halo, halo),
         in_specs=[hbm] * 4,
-        out_specs=[vmem] + [hbm] * 2,
+        out_specs=[hbm] * 3,
         scratch_shapes=[
+            pltpu.VMEM((everyone, LANES), f32),
             pltpu.VMEM((n_rows, wide), f32),
             pltpu.VMEM(offsets_x.shape, jnp.int32),
             pltpu.VMEM((1, LANES), f32),
             pltpu.SemaphoreType.DMA((6,)),
-            pltpu.SemaphoreType.DMA((2,)),
+            pltpu.SemaphoreType.DMA((3,)),
         ],
         compiler_params=pltpu.CompilerParams(vmem_limit_bytes=A_LIMIT),
     )(density, velocity, pressure, offsets_x)

time: 37 us -> 36.3 us (0.981)
  Pallas kernels: 8.85 us -> 8.18 us
    pallas_call x1, Pallas kernels: 2.6 us -> 2.01 us  [body(): pl.pallas_call(speed_kernel, out_shape=(jax.ShapeDtypeStruct((everyone, L...]
where the time goes in v2:
time: 36.3 us; the launch traced here: 36 us
  starting transfers between devices  18 us (50%)
  Pallas kernels  8.18 us (23%)
  waiting for transfers between devices  5.06 us (14%)
  local copies, waits for them, and re-layouts  4.14 us (11%)
  between operations  0.67 us (2%)
    all_to_all x1, starting transfers between devices, body(): lax.all_to_all(pay, ('rows', 'cols'), split_axis=0, concat_axis=0, tiled=...  15.7 us
    pallas_call x1, Pallas kernels, body(): pl.pallas_call(sweep_kernel, out_shape=(plane, jax.ShapeDtypeStruct(veloc...  4.69 us
    all_to_all x1, waiting for transfers between devices, body(): lax.all_to_all(pay, ('rows', 'cols'), split_axis=0, concat_axis=0, tiled=...  4.4 us
    unnamed x10, local copies, waits for them, and re-layouts  4.14 us
    pallas_call x1, Pallas kernels, body(): pl.pallas_call(speed_kernel, out_shape=(jax.ShapeDtypeStruct((everyone, L...  2.01 us
    ppermute x1, starting transfers between devices, body(): lax.ppermute(up, 'rows', [(i, (i + 1) % n_dev) for i in range(n_dev)])  1.83 us
    pallas_call x1, Pallas kernels, body(): pl.pallas_call(own_kernel, out_shape=(jax.ShapeDtypeStruct((9, n_own * SU...  0.94 us
  transfers between devices with their start and end apart: 3, of which 2 were waited for; matrix products, arithmetic and copies ran while one was open for 0% of the time, Pallas kernels for 4%

profile of v2, /device:TPU:1, one launch (start us, length us, event | category | flops | bytes accessed | tf_op | source)
XLA Modules:
  0.0 36.0 jit_solution(18356624827261170727)
XLA Ops:
  0.6 2.0 %shard_map.77 = (f32[256,128]{1,0:T(8,128)}, f32[8,5248]{1,0:T(8,128)}, f32[8,5248]{1,0:T(8,128)}) custom-call(f32[1,32,1024]{2,1,0:T(8,128)} %den.3, f32[3,1,32,1024]{3,2,1,0:T(8,128)} %vel.3, f32[1,32,1024]{2,1,0:T(8,128)} %prs.3, s32[1,32]{1,0:T(1,128)} %offx_hbm.1), custom_call_target="tpu_custom_call" | custom-call | tf_op jit(solution)/shard_map/pallas_call | solution.py:408
  2.6 15.7 %all-to-all-start = ((f32[256,1,128]{2,1,0:T(1,128)}), f32[256,1,128]{2,1,0:T(1,128)S(1)}, u32[]{:S(2)}, u32[]{:S(2)}) async-start(f32[256,1,128]{2,1,0:T(1,128)} %bitcast.5), calls=%async_computation | async-start | bytes 262144 | tf_op jit(solution)/shard_map/all_to_all | solution.py:423
  18.3 1.8 %collective-permute-start = (f32[8,5248]{1,0:T(8,128)}, f32[8,5248]{1,0:T(8,128)S(1)}, u32[]{:S(2)}, u32[]{:S(2)}) collective-permute-start(f32[8,5248]{1,0:T(8,128)} %get-tuple-element.12), channel_id=1, source_target_pairs={{0,8},{8,16},{16,24},{24,32},{32,40},{40,48},{48,56},{56,64},{64,7... | collective-permute-start | bytes 503816 | tf_op jit(solution)/shard_map/ppermute | solution.py:424
  20.1 0.5 %collective-permute-start.1 = (f32[8,5248]{1,0:T(8,128)}, f32[8,5248]{1,0:T(8,128)S(1)}, u32[]{:S(2)}, u32[]{:S(2)}) collective-permute-start(f32[8,5248]{1,0:T(8,128)} %get-tuple-element.13), channel_id=1, source_target_pairs={{0,248},{8,0},{16,8},{24,16},{32,24},{40,32},{48,40},{56,48},{64,5... | collective-permute-start | bytes 503816 | tf_op jit(solution)/shard_map/ppermute | solution.py:425
  20.6 0.0 copy-start
  20.6 1.0 %copy-done = f32[3,1,32,1024]{3,2,1,0:T(8,128)S(1)} copy-done((f32[3,1,32,1024]{3,2,1,0:T(8,128)S(1)}, f32[3,1,32,1024]{3,2,1,0:T(8,128)}, u32[]{:S(2)}) %copy-start) | copy-done | bytes 393240
  21.6 0.0 copy-start.1
  21.6 0.9 %copy-done.1 = f32[1,32,1024]{2,1,0:T(8,128)S(1)} copy-done((f32[1,32,1024]{2,1,0:T(8,128)S(1)}, f32[1,32,1024]{2,1,0:T(8,128)}, u32[]{:S(2)}) %copy-start.1) | copy-done | bytes 131096
  22.5 0.0 copy-start.2
  22.5 0.9 %copy-done.2 = f32[1,32,1024]{2,1,0:T(8,128)S(1)} copy-done((f32[1,32,1024]{2,1,0:T(8,128)S(1)}, f32[1,32,1024]{2,1,0:T(8,128)}, u32[]{:S(2)}) %copy-start.2) | copy-done | bytes 131096
  23.4 0.0 copy-start.3
  23.4 0.7 %copy-done.3 = s32[1,1024]{1,0:T(1,128)S(1)} copy-done((s32[1,1024]{1,0:T(1,128)S(1)}, s32[1,1024]{1,0:T(1,128)}, u32[]{:S(2)}) %copy-start.3) | copy-done | bytes 4120
  24.1 0.0 copy-start.4
  24.1 0.7 %copy-done.4 = s32[1,32]{1,0:T(1,128)S(1)} copy-done((s32[1,32]{1,0:T(1,128)S(1)}, s32[1,32]{1,0:T(1,128)}, u32[]{:S(2)}) %copy-start.4) | copy-done | bytes 152
  24.8 0.9 %shard_map.76 = (f32[9,16,2816]{2,1,0:T(8,128)S(1)}, f32[16,128]{1,0:T(8,128)S(1)}, f32[8,128]{1,0:T(8,128)S(1)}) custom-call(f32[1,32,1024]{2,1,0:T(8,128)S(1)} %copy-done.1, f32[3,1,32,1024]{3,2,1,0:T(8,128)S(1)} %copy-done, f32[1,32,1024]{2,1,0:T(8,128)S(1)} %copy-done.2, s32[1,32]{1,0:T(1,128)S(1)} %copy-done.4, s32[1,1024]{1,0:T(1,128)S(1)} %copy-done.3), custom_call_target="tpu_custom_call" | custom-call | flops 1000000 | bytes 1000000 | tf_op jit(solution)/shard_map/pallas_call | solution.py:429
  25.7 0.0 collective-permute-done.before
  25.7 0.7 %collective-permute-done.1.after = f32[8,5248]{1,0:T(8,128)S(1)} collective-permute-done((f32[8,5248]{1,0:T(8,128)}, f32[8,5248]{1,0:T(8,128)S(1)}, u32[]{:S(2)}, u32[]{:S(2)}) %collective-permute-start.1) | collective-permute-done | bytes 167968 | tf_op jit(solution)/shard_map/ppermute | solution.py:425
  26.4 0.5 %shard_map.78 = (f32[9,8,2816]{2,1,0:T(8,128)S(1)}, f32[8,128]{1,0:T(8,128)S(1)}) custom-call(f32[8,5248]{1,0:T(8,128)S(1)} %collective-permute-done.before, f32[8,5248]{1,0:T(8,128)S(1)} %collective-permute-done.1.after), custom_call_target="tpu_custom_call" | custom-call | flops 1000000 | bytes 1000000 | tf_op jit(solution)/shard_map/pallas_call | solution.py:442
  26.9 4.4 %all-to-all-done = f32[256,1,128]{2,1,0:T(1,128)S(1)} async-done(((f32[256,1,128]{2,1,0:T(1,128)}), f32[256,1,128]{2,1,0:T(1,128)S(1)}, u32[]{:S(2)}, u32[]{:S(2)}) %all-to-all-start) | async-done | bytes 131104 | tf_op jit(solution)/shard_map/all_to_all | solution.py:423
  31.3 4.7 %shard_map.79 = (f32[1,32,1024]{2,1,0:T(8,128)}, f32[3,1,32,1024]{3,2,1,0:T(8,128)}, f32[1,32,1024]{2,1,0:T(8,128)}) custom-call(f32[9,16,2816]{2,1,0:T(8,128)S(1)} %get-tuple-element.11.state, f32[9,8,2816]{2,1,0:T(8,128)S(1)} %get-tuple-element.14.halo_state, f32[256,128]{1,0:T(8,128)S(1)} %bitcast.4, f32[16,128]{1,0:T(8,128)S(1)} %get-tuple-element.16.rows_by, ...), custom_call_target="tpu_custom_call" | custom-call | tf_op jit(solution)/shard_map/pallas_call | solution.py:456
Async XLA Ops:
  2.6 28.7 %all-to-all-start = ((f32[256,1,128]{2,1,0:T(1,128)}), f32[256,1,128]{2,1,0:T(1,128)S(1)}, u32[]{:S(2)}, u32[]{:S(2)}) async-start(f32[256,1,128]{2,1,0:T(1,128)} %bitcast.5), calls=%async_computation | async-start | bytes 262144 | tf_op jit(solution)/shard_map/all_to_all | solution.py:423
  18.3 7.4 %collective-permute-start = (f32[8,5248]{1,0:T(8,128)}, f32[8,5248]{1,0:T(8,128)S(1)}, u32[]{:S(2)}, u32[]{:S(2)}) collective-permute-start(f32[8,5248]{1,0:T(8,128)} %get-tuple-element.12), channel_id=1, source_target_pairs={{0,8},{8,16},{16,24},{24,32},{32,40},{40,48},{48,56},{56,64},{64,7... | collective-permute-start | bytes 503816 | tf_op jit(solution)/shard_map/ppermute | solution.py:424
  20.1 6.2 %collective-permute-start.1 = (f32[8,5248]{1,0:T(8,128)}, f32[8,5248]{1,0:T(8,128)S(1)}, u32[]{:S(2)}, u32[]{:S(2)}) collective-permute-start(f32[8,5248]{1,0:T(8,128)} %get-tuple-element.13), channel_id=1, source_target_pairs={{0,248},{8,0},{16,8},{24,16},{32,24},{40,32},{48,40},{56,48},{64,5... | collective-permute-start | bytes 503816 | tf_op jit(solution)/shard_map/ppermute | solution.py:425
  20.6 1.0 %copy-start = (f32[3,1,32,1024]{3,2,1,0:T(8,128)S(1)}, f32[3,1,32,1024]{3,2,1,0:T(8,128)}, u32[]{:S(2)}) copy-start(f32[3,1,32,1024]{3,2,1,0:T(8,128)} %vel.3) | copy-start | bytes 1179652
  21.6 0.9 %copy-start.1 = (f32[1,32,1024]{2,1,0:T(8,128)S(1)}, f32[1,32,1024]{2,1,0:T(8,128)}, u32[]{:S(2)}) copy-start(f32[1,32,1024]{2,1,0:T(8,128)} %den.3) | copy-start | bytes 393220
  22.5 0.9 %copy-start.2 = (f32[1,32,1024]{2,1,0:T(8,128)S(1)}, f32[1,32,1024]{2,1,0:T(8,128)}, u32[]{:S(2)}) copy-start(f32[1,32,1024]{2,1,0:T(8,128)} %prs.3) | copy-start | bytes 393220
  23.4 0.7 %copy-start.3 = (s32[1,1024]{1,0:T(1,128)S(1)}, s32[1,1024]{1,0:T(1,128)}, u32[]{:S(2)}) copy-start(s32[1,1024]{1,0:T(1,128)} %offy.1) | copy-start | bytes 12292
  24.1 0.7 %copy-start.4 = (s32[1,32]{1,0:T(1,128)S(1)}, s32[1,32]{1,0:T(1,128)}, u32[]{:S(2)}) copy-start(s32[1,32]{1,0:T(1,128)} %offx_hbm.1) | copy-start | bytes 388

commit v3 on v2

--- a/solution.py
+++ b/solution.py
@@ -7,11 +7,11 @@
 
 SHIFT = 2
 PAIR = 16
-REACH = 3
+REACH = 2
 A_LIMIT = 60 * 2**20
 OWN_COST = 10**6
 HALO_COST = 10**6
-LEAD = 16
+LEAD = 10
 HALO = 8
 LANES = 128
 SUB = 8
@@ -57,8 +57,26 @@
 
 def flux_weights(d, f):
     rest = 1.0 - f
-    df = d * f
-    return d * rest * rest, df * (3.0 - 2.0 * f), df * rest
+    near = d * rest
+    return near * rest, f * near
+
+
+def gaps_of(gap, step, gap_before, step_before):
+    left = gap_before - step_before
+    return clamp(left, 0.0, -2.0 * gap), clamp(gap, 0.0, -2.0 * left)
+
+
+def step_and_gap(before, a, after, after2):
+    step = after - a
+    gap = 0.5 * step + (1.0 / 12.0) * ((a - before) - (after2 - after))
+    return step, clamp(gap, 0.0, step)
+
+
+def flux_of(up, d, k_near, k_far, a, gaps, a_next, gaps_next):
+    (low, high), (low_next, high_next) = gaps, gaps_next
+    near = jnp.where(up, high, low_next)
+    far = jnp.where(up, low, high_next)
+    return d * jnp.where(up, a, a_next) + k_near * near - k_far * far
 
 
 def primitive(mass, mn, ma, mb, energy):
@@ -137,7 +155,8 @@
     tiles = split(peak)
     while len(tiles) > 1:
         tiles = [jnp.maximum(x, y) for x, y in zip(tiles[::2], tiles[1::2])]
-    pay[...] = jnp.broadcast_to(jnp.max(tiles[0], axis=0, keepdims=True), pay.shape)
+    top = jnp.max(jnp.max(tiles[0], axis=0, keepdims=True), axis=1, keepdims=True)
+    pay[...] = jnp.broadcast_to(top, pay.shape)
     packs.append(pltpu.make_async_copy(pay, pay_hbm, pack_sems.at[2]))
     packs[-1].start()
     for pack in packs:
@@ -201,7 +220,7 @@
     top = [got[k * SUB : (k + 1) * SUB, :] for k in range(got.shape[0] // SUB)]
     while len(top) > 1:
         top = [jnp.maximum(x, y) for x, y in zip(top[::2], top[1::2])]
-    dt = courant / jnp.max(jnp.max(top[0], axis=0, keepdims=True), axis=1, keepdims=True)
+    dt = courant / jnp.max(top[0], axis=0, keepdims=True)
 
     def x_group(state, row, offsets, block, late):
         o = pl.ds(row, SUB)
@@ -209,57 +228,74 @@
         def tile_of(n, t):
             return state[n, o, (t + REACH) * LANES : (t + REACH + 1) * LANES]
 
-        width, inv_w, amount, face, edges, flux, result = {}, {}, {}, {}, {}, {}, {}
-        shifted = {k: offsets == k for k in range(-SHIFT, SHIFT + 1) if k}
+        width, inv_w, amount, step, face, gaps, flux, result = {}, {}, {}, {}, {}, {}, {}, {}
+        bits = offsets + float(SHIFT)
+        high_bit = bits > 3.5
+        low_bits = jnp.where(high_bit, 0.0, bits)
+        mid_bit = low_bits > 1.5
+        odd = low_bits - jnp.where(mid_bit, 2.0, 0.0) > 0.5
+        once = {}
+
+        def moved_one(j, f):
+            if (j, f) not in once:
+                once[j, f] = jnp.where(odd, result[j - 1][f], result[j][f])
+            return once[j, f]
 
         def put(j):
             for f in range(5):
-                v = result[j][f]
-                for k, mask in shifted.items():
-                    v = jnp.where(mask, result[j - k][f], v)
+                v = jnp.where(mid_bit, moved_one(j, f), moved_one(j + 2, f))
+                v = jnp.where(high_bit, result[j - 2][f], v)
                 columns[block, f, pl.ds(j, SUB, stride=n_steps), :] = v
 
-        for t in range(-REACH, n_steps + REACH):
-            width[t] = 1.0 + dt * tile_of(2, t)
-            inv_w[t] = inverse(width[t])
-            lag = tile_of(0, t) * inv_w[t]
-            amount[t] = (
-                lag, lag * (tile_of(3, t) - dt * tile_of(4, t)), lag * tile_of(5, t), lag * tile_of(6, t),
-                lag * (tile_of(7, t) - dt * tile_of(8, t)),
-            )
+        def finish(i):
+            kept = [tile_of(0, i)] + [amount[i][f] * width[i] for f in range(1, 5)]
+            result[i] = primitive(*(kept[f] + flux[i - 1][f] - flux[i][f] for f in range(5)))
+            if i < SHIFT:
+                result[n_steps + i] = [wrapped(v, -1) for v in result[i]]
+            if i >= n_steps - SHIFT:
+                result[i - n_steps] = [wrapped(v, 1) for v in result[i]]
+
+        def first():
+            flux[-1] = [wrapped(v, 1) for v in flux[n_steps - 1]]
+            finish(0)
+
+        for t in range(-REACH, n_steps + 3):
+            if t < n_steps + REACH:
+                width[t] = 1.0 + dt * tile_of(2, t)
+                inv_w[t] = inverse(width[t])
+                lag = tile_of(0, t) * inv_w[t]
+                amount[t] = (
+                    lag, lag * (tile_of(3, t) - dt * tile_of(4, t)), lag * tile_of(5, t), lag * tile_of(6, t),
+                    lag * (tile_of(7, t) - dt * tile_of(8, t)),
+                )
             if late:
                 late.pop(0)()
             i = t - 2
-            n = t - 3
-            if n >= -1:
-                us = tile_of(1, n)
+            c = t - 3
+            if c >= 0:
+                us = tile_of(1, c)
                 up = us > 0.0
                 d = dt * us
-                k1, k2, k3 = flux_weights(d, jnp.abs(d) * jnp.where(up, inv_w[n], inv_w[n + 1]))
-                flux[n] = []
-            face[i], edges[i] = [], []
+                weights = flux_weights(d, jnp.abs(d) * jnp.where(up, inv_w[c], inv_w[c + 1]))
+                flux[c] = []
+            step[i], face[i], gaps[i] = [], [], []
             for f in range(5):
-                if i >= -2:
-                    face[i].append(face_of(*(amount[i + k][f] for k in (-1, 0, 1, 2))))
-                if i >= -1:
-                    edges[i].append(edges_of(amount[i][f], face[i - 1][f], face[i][f]))
-                if n >= -1:
-                    (low, high), (low_n, high_n) = edges[n][f], edges[n + 1][f]
-                    near = jnp.where(up, high, low_n)
-                    far = jnp.where(up, low, high_n)
-                    mean = jnp.where(up, amount[n][f], amount[n + 1][f])
-                    flux[n].append(k1 * near + k2 * mean - k3 * far)
-            i = n
-            if i >= 0:
-                kept = [tile_of(0, i)] + [amount[i][f] * width[i] for f in range(1, 5)]
-                result[i] = primitive(*(kept[f] + flux[i - 1][f] - flux[i][f] for f in range(5)))
-                if i < SHIFT:
-                    result[n_steps + i] = [wrapped(v, -1) for v in result[i]]
-                if i >= n_steps - SHIFT:
-                    result[i - n_steps] = [wrapped(v, 1) for v in result[i]]
-                if i >= 2 * SHIFT:
-                    put(i - SHIFT)
-        for j in (n_steps - 2, n_steps - 1, 0, 1):
+                if -1 <= i < n_steps:
+                    steps = step_and_gap(*(amount[i + k][f] for k in (-1, 0, 1, 2)))
+                    step[i].append(steps[0])
+                    face[i].append(steps[1])
+                if 0 <= i < n_steps:
+                    gaps[i].append(gaps_of(face[i][f], step[i][f], face[i - 1][f], step[i - 1][f]))
+                if i == n_steps:
+                    gaps[i].append([wrapped(v, -1) for v in gaps[0][f]])
+                if c >= 0:
+                    flux[c].append(flux_of(up, d, *weights, amount[c][f], gaps[c][f], amount[c + 1][f], gaps[c + 1][f]))
+            if c >= 1:
+                finish(c)
+                if c >= 2 * SHIFT + 1:
+                    put(c - SHIFT)
+        late.append(first)
+        for j in (n_steps - 2, n_steps - 1, 0, 1, 2):
             late.append(lambda j=j: put(j))
 
     def turn(n, f, first, second):
@@ -291,10 +327,20 @@
         rho, ta, un, tb, p = (swept[f, pl.ds(at, SUB, stride=SUB), :] for f in range(5))
         return rho, un, ta, tb, p
 
-    oy = lines_by[...]
-    moved = {k: oy == k for k in range(-SHIFT, SHIFT + 1) if k}
+    bits = lines_by[...] + float(SHIFT)
+    high_bit = bits > 3.5
+    low_bits = jnp.where(high_bit, 0.0, bits)
+    mid_bit = low_bits > 1.5
+    odd = low_bits - jnp.where(mid_bit, 2.0, 0.0) > 0.5
+    once = {}
+
+    def moved_one(i, f):
+        if (i, f) not in once:
+            once[i, f] = jnp.where(odd, done[i - 1][f], done[i][f])
+        return once[i, f]
+
     cells, inv_rho, imp, faces, edges = {}, {}, {}, {}, {}
-    stars, lags, weights, q_faces, q_edges, fluxes, done = {}, {}, {}, {}, {}, {}, {}
+    stars, lags, weights, q_steps, q_faces, q_edges, fluxes, done = {}, {}, {}, {}, {}, {}, {}, {}
     copies, waiting = [], []
     targets = (den_out.at[0], vel_out.at[1, 0], vel_out.at[0, 0], vel_out.at[2, 0], prs_out.at[0])
 
@@ -304,13 +350,10 @@
         for k, tile in enumerate(tiles):
             tiles_out[f, here, pl.ds(k * LANES, LANES)] = tile
 
-    def send(a):
+    def send(a, f):
         here = pl.ds(a * SUB, SUB)
-        for f in range(5):
-            copies.append(
-                pltpu.make_async_copy(tiles_out.at[f, here, :], targets[f].at[here, :], out_sem.at[f, a])
-            )
-            copies[-1].start()
+        copies.append(pltpu.make_async_copy(tiles_out.at[f, here, :], targets[f].at[here, :], out_sem.at[f, a]))
+        copies[-1].start()
 
     def solve_row(r):
         if turns:
@@ -350,36 +393,40 @@
         if n >= 5:
             d = stars[n][3]
             up = d > 0.0
-            k1, k2, k3 = flux_weights(d, jnp.abs(d) * jnp.where(up, weights[n][1], weights[n + 1][1]))
+            near_far = flux_weights(d, jnp.abs(d) * jnp.where(up, weights[n][1], weights[n + 1][1]))
             fluxes[n] = []
-        q_faces[i], q_edges[i] = [], []
+        q_steps[i], q_faces[i], q_edges[i] = [], [], []
         for f in range(5):
             if i >= 4:
-                q_faces[i].append(face_of(*(lags[i + k][f] for k in (-1, 0, 1, 2))))
+                step, face = step_and_gap(*(lags[i + k][f] for k in (-1, 0, 1, 2)))
+                q_steps[i].append(step)
+                q_faces[i].append(face)
             if i >= 5:
-                q_edges[i].append(edges_of(lags[i][f], q_faces[i - 1][f], q_faces[i][f]))
+                q_edges[i].append(gaps_of(q_faces[i][f], q_steps[i][f], q_faces[i - 1][f], q_steps[i - 1][f]))
             if n >= 5:
-                (low, high), (low_n, high_n) = q_edges[n][f], q_edges[n + 1][f]
-                near = jnp.where(up, high, low_n)
-                far = jnp.where(up, low, high_n)
-                fluxes[n].append(k1 * near + k2 * jnp.where(up, lags[n][f], lags[n + 1][f]) - k3 * far)
+                fluxes[n].append(
+                    flux_of(up, d, *near_far, lags[n][f], q_edges[n][f], lags[n + 1][f], q_edges[n + 1][f])
+                )
         i = n
         if i >= 6:
             done[i] = primitive(
-                *(lags[i][f] * weights[i][0] + fluxes[i - 1][f] - fluxes[i][f] for f in range(5))
+                *(
+                    (lags[i][f] * weights[i][0] if f else cells[i][0]) + fluxes[i - 1][f] - fluxes[i][f]
+                    for f in range(5)
+                )
             )
         i = r - 8
         if i >= HALO:
             j = i - HALO
             a, b = divmod(j, SUB)
             for f in range(5):
-                v = done[i][f]
-                for k, mask in moved.items():
-                    v = jnp.where(mask, done[i - k][f], v)
+                v = jnp.where(mid_bit, moved_one(i, f), moved_one(i + 2, f))
+                v = jnp.where(high_bit, done[i - 2][f], v)
                 rows_out[f, pl.ds(a * n_tiles * SUB + b, SUB, stride=SUB), :] = v
             if b == SUB - 1:
                 if a:
-                    send(a - 1)
+                    for f in range(5):
+                        send(a - 1, f)
                 waiting.extend((a, f) for f in range(5))
         if waiting:
             turn_back(*waiting.pop(0))
@@ -389,9 +436,10 @@
             solve_row(r)
         if r >= LEAD:
             remap_row(r - LEAD)
-    for a, f in waiting:
-        turn_back(a, f)
-    send(n_rows // SUB - 1)
+    for f in range(5):
+        if (n_rows // SUB - 1, f) in waiting:
+            turn_back(n_rows // SUB - 1, f)
+        send(n_rows // SUB - 1, f)
     for copy in copies:
         copy.wait()
 

time: 36.3 us -> 35.9 us (0.989)
  Pallas kernels: 8.18 us -> 7.68 us
    pallas_call x1, Pallas kernels: 4.69 us -> 4.23 us  [body(): pl.pallas_call(sweep_kernel, out_shape=(plane, jax.ShapeDtypeStruct(veloc...]
where the time goes in v3:
time: 35.9 us; the launch traced here: 35.6 us
  starting transfers between devices  18 us (50%)
  Pallas kernels  7.68 us (21%)
  waiting for transfers between devices  5.17 us (14%)
  local copies, waits for them, and re-layouts  4.14 us (12%)
  between operations  0.66 us (2%)
    all_to_all x1, starting transfers between devices, body(): lax.all_to_all(pay, ('rows', 'cols'), split_axis=0, concat_axis=0, tiled=...  15.7 us
    all_to_all x1, waiting for transfers between devices, body(): lax.all_to_all(pay, ('rows', 'cols'), split_axis=0, concat_axis=0, tiled=...  4.34 us
    pallas_call x1, Pallas kernels, body(): pl.pallas_call(sweep_kernel, out_shape=(plane, jax.ShapeDtypeStruct(veloc...  4.23 us
    unnamed x10, local copies, waits for them, and re-layouts  4.14 us
    pallas_call x1, Pallas kernels, body(): pl.pallas_call(speed_kernel, out_shape=(jax.ShapeDtypeStruct((everyone, L...  2.06 us
    ppermute x1, starting transfers between devices, body(): lax.ppermute(up, 'rows', [(i, (i + 1) % n_dev) for i in range(n_dev)])  1.83 us
    ppermute x1, waiting for transfers between devices, body(): lax.ppermute(down, 'rows', [(i, (i - 1) % n_dev) for i in range(n_dev)])  0.83 us
    pallas_call x1, Pallas kernels, body(): pl.pallas_call(own_kernel, out_shape=(jax.ShapeDtypeStruct((9, n_own * SU...  0.78 us
  transfers between devices with their start and end apart: 3, of which 2 were waited for; matrix products, arithmetic and copies ran while one was open for 0% of the time, Pallas kernels for 4%

profile of v3, /device:TPU:1, one launch (start us, length us, event | category | flops | bytes accessed | tf_op | source)
XLA Modules:
  0.0 35.6 jit_solution(736185086234117963)
XLA Ops:
  0.6 2.1 %shard_map.77 = (f32[256,128]{1,0:T(8,128)}, f32[8,5248]{1,0:T(8,128)}, f32[8,5248]{1,0:T(8,128)}) custom-call(f32[1,32,1024]{2,1,0:T(8,128)} %den.3, f32[3,1,32,1024]{3,2,1,0:T(8,128)} %vel.3, f32[1,32,1024]{2,1,0:T(8,128)} %prs.3, s32[1,32]{1,0:T(1,128)} %offx_hbm.1), custom_call_target="tpu_custom_call" | custom-call | tf_op jit(solution)/shard_map/pallas_call | solution.py:456
  2.7 15.7 %all-to-all-start = ((f32[256,1,128]{2,1,0:T(1,128)}), f32[256,1,128]{2,1,0:T(1,128)S(1)}, u32[]{:S(2)}, u32[]{:S(2)}) async-start(f32[256,1,128]{2,1,0:T(1,128)} %bitcast.5), calls=%async_computation | async-start | bytes 262144 | tf_op jit(solution)/shard_map/all_to_all | solution.py:471
  18.4 1.8 %collective-permute-start = (f32[8,5248]{1,0:T(8,128)}, f32[8,5248]{1,0:T(8,128)S(1)}, u32[]{:S(2)}, u32[]{:S(2)}) collective-permute-start(f32[8,5248]{1,0:T(8,128)} %get-tuple-element.12), channel_id=1, source_target_pairs={{0,8},{8,16},{16,24},{24,32},{32,40},{40,48},{48,56},{56,64},{64,7... | collective-permute-start | bytes 503816 | tf_op jit(solution)/shard_map/ppermute | solution.py:472
  20.2 0.5 %collective-permute-start.1 = (f32[8,5248]{1,0:T(8,128)}, f32[8,5248]{1,0:T(8,128)S(1)}, u32[]{:S(2)}, u32[]{:S(2)}) collective-permute-start(f32[8,5248]{1,0:T(8,128)} %get-tuple-element.13), channel_id=1, source_target_pairs={{0,248},{8,0},{16,8},{24,16},{32,24},{40,32},{48,40},{56,48},{64,5... | collective-permute-start | bytes 503816 | tf_op jit(solution)/shard_map/ppermute | solution.py:473
  20.7 0.0 copy-start
  20.7 1.0 %copy-done = f32[3,1,32,1024]{3,2,1,0:T(8,128)S(1)} copy-done((f32[3,1,32,1024]{3,2,1,0:T(8,128)S(1)}, f32[3,1,32,1024]{3,2,1,0:T(8,128)}, u32[]{:S(2)}) %copy-start) | copy-done | bytes 393240
  21.7 0.0 copy-start.1
  21.7 0.9 %copy-done.1 = f32[1,32,1024]{2,1,0:T(8,128)S(1)} copy-done((f32[1,32,1024]{2,1,0:T(8,128)S(1)}, f32[1,32,1024]{2,1,0:T(8,128)}, u32[]{:S(2)}) %copy-start.1) | copy-done | bytes 131096
  22.6 0.0 copy-start.2
  22.6 0.9 %copy-done.2 = f32[1,32,1024]{2,1,0:T(8,128)S(1)} copy-done((f32[1,32,1024]{2,1,0:T(8,128)S(1)}, f32[1,32,1024]{2,1,0:T(8,128)}, u32[]{:S(2)}) %copy-start.2) | copy-done | bytes 131096
  23.5 0.0 copy-start.3
  23.5 0.7 %copy-done.3 = s32[1,1024]{1,0:T(1,128)S(1)} copy-done((s32[1,1024]{1,0:T(1,128)S(1)}, s32[1,1024]{1,0:T(1,128)}, u32[]{:S(2)}) %copy-start.3) | copy-done | bytes 4120
  24.2 0.0 copy-start.4
  24.2 0.7 %copy-done.4 = s32[1,32]{1,0:T(1,128)S(1)} copy-done((s32[1,32]{1,0:T(1,128)S(1)}, s32[1,32]{1,0:T(1,128)}, u32[]{:S(2)}) %copy-start.4) | copy-done | bytes 152
  24.8 0.8 %shard_map.76 = (f32[9,16,2560]{2,1,0:T(8,128)S(1)}, f32[16,128]{1,0:T(8,128)S(1)}, f32[8,128]{1,0:T(8,128)S(1)}) custom-call(f32[1,32,1024]{2,1,0:T(8,128)S(1)} %copy-done.1, f32[3,1,32,1024]{3,2,1,0:T(8,128)S(1)} %copy-done, f32[1,32,1024]{2,1,0:T(8,128)S(1)} %copy-done.2, s32[1,32]{1,0:T(1,128)S(1)} %copy-done.4, s32[1,1024]{1,0:T(1,128)S(1)} %copy-done.3), custom_call_target="tpu_custom_call" | custom-call | flops 1000000 | bytes 1000000 | tf_op jit(solution)/shard_map/pallas_call | solution.py:477
  25.6 0.0 collective-permute-done.before
  25.6 0.8 %collective-permute-done.1.after = f32[8,5248]{1,0:T(8,128)S(1)} collective-permute-done((f32[8,5248]{1,0:T(8,128)}, f32[8,5248]{1,0:T(8,128)S(1)}, u32[]{:S(2)}, u32[]{:S(2)}) %collective-permute-start.1) | collective-permute-done | bytes 167968 | tf_op jit(solution)/shard_map/ppermute | solution.py:473
  26.4 0.6 %shard_map.78 = (f32[9,8,2560]{2,1,0:T(8,128)S(1)}, f32[8,128]{1,0:T(8,128)S(1)}) custom-call(f32[8,5248]{1,0:T(8,128)S(1)} %collective-permute-done.before, f32[8,5248]{1,0:T(8,128)S(1)} %collective-permute-done.1.after), custom_call_target="tpu_custom_call" | custom-call | flops 1000000 | bytes 1000000 | tf_op jit(solution)/shard_map/pallas_call | solution.py:490
  27.1 4.3 %all-to-all-done = f32[256,1,128]{2,1,0:T(1,128)S(1)} async-done(((f32[256,1,128]{2,1,0:T(1,128)}), f32[256,1,128]{2,1,0:T(1,128)S(1)}, u32[]{:S(2)}, u32[]{:S(2)}) %all-to-all-start) | async-done | bytes 131104 | tf_op jit(solution)/shard_map/all_to_all | solution.py:471
  31.4 4.2 %shard_map.79 = (f32[1,32,1024]{2,1,0:T(8,128)}, f32[3,1,32,1024]{3,2,1,0:T(8,128)}, f32[1,32,1024]{2,1,0:T(8,128)}) custom-call(f32[9,16,2560]{2,1,0:T(8,128)S(1)} %get-tuple-element.11.state, f32[9,8,2560]{2,1,0:T(8,128)S(1)} %get-tuple-element.14.halo_state, f32[256,128]{1,0:T(8,128)S(1)} %bitcast.4, f32[16,128]{1,0:T(8,128)S(1)} %get-tuple-element.16.rows_by, ...), custom_call_target="tpu_custom_call" | custom-call | tf_op jit(solution)/shard_map/pallas_call | solution.py:504
Async XLA Ops:
  2.7 28.7 %all-to-all-start = ((f32[256,1,128]{2,1,0:T(1,128)}), f32[256,1,128]{2,1,0:T(1,128)S(1)}, u32[]{:S(2)}, u32[]{:S(2)}) async-start(f32[256,1,128]{2,1,0:T(1,128)} %bitcast.5), calls=%async_computation | async-start | bytes 262144 | tf_op jit(solution)/shard_map/all_to_all | solution.py:471
  18.4 7.2 %collective-permute-start = (f32[8,5248]{1,0:T(8,128)}, f32[8,5248]{1,0:T(8,128)S(1)}, u32[]{:S(2)}, u32[]{:S(2)}) collective-permute-start(f32[8,5248]{1,0:T(8,128)} %get-tuple-element.12), channel_id=1, source_target_pairs={{0,8},{8,16},{16,24},{24,32},{32,40},{40,48},{48,56},{56,64},{64,7... | collective-permute-start | bytes 503816 | tf_op jit(solution)/shard_map/ppermute | solution.py:472
  20.2 6.2 %collective-permute-start.1 = (f32[8,5248]{1,0:T(8,128)}, f32[8,5248]{1,0:T(8,128)S(1)}, u32[]{:S(2)}, u32[]{:S(2)}) collective-permute-start(f32[8,5248]{1,0:T(8,128)} %get-tuple-element.13), channel_id=1, source_target_pairs={{0,248},{8,0},{16,8},{24,16},{32,24},{40,32},{48,40},{56,48},{64,5... | collective-permute-start | bytes 503816 | tf_op jit(solution)/shard_map/ppermute | solution.py:473
  20.7 1.0 %copy-start = (f32[3,1,32,1024]{3,2,1,0:T(8,128)S(1)}, f32[3,1,32,1024]{3,2,1,0:T(8,128)}, u32[]{:S(2)}) copy-start(f32[3,1,32,1024]{3,2,1,0:T(8,128)} %vel.3) | copy-start | bytes 1179652
  21.7 0.9 %copy-start.1 = (f32[1,32,1024]{2,1,0:T(8,128)S(1)}, f32[1,32,1024]{2,1,0:T(8,128)}, u32[]{:S(2)}) copy-start(f32[1,32,1024]{2,1,0:T(8,128)} %den.3) | copy-start | bytes 393220
  22.6 0.9 %copy-start.2 = (f32[1,32,1024]{2,1,0:T(8,128)S(1)}, f32[1,32,1024]{2,1,0:T(8,128)}, u32[]{:S(2)}) copy-start(f32[1,32,1024]{2,1,0:T(8,128)} %prs.3) | copy-start | bytes 393220
  23.5 0.7 %copy-start.3 = (s32[1,1024]{1,0:T(1,128)S(1)}, s32[1,1024]{1,0:T(1,128)}, u32[]{:S(2)}) copy-start(s32[1,1024]{1,0:T(1,128)} %offy.1) | copy-start | bytes 12292
  24.2 0.7 %copy-start.4 = (s32[1,32]{1,0:T(1,128)S(1)}, s32[1,32]{1,0:T(1,128)}, u32[]{:S(2)}) copy-start(s32[1,32]{1,0:T(1,128)} %offx_hbm.1) | copy-start | bytes 388

commit v4 on v3

--- a/solution.py
+++ b/solution.py
@@ -131,7 +131,12 @@
     n_rows, n_x = den.shape[1:]
     off_load = pltpu.make_async_copy(offx_hbm, offx, sems.at[5])
     sources = (den.at[0], vel.at[0, 0], vel.at[1, 0], vel.at[2, 0], prs.at[0])
-    loads = [pltpu.make_async_copy(sources[f], block.at[:, pl.ds(f * n_x, n_x)], sems.at[f]) for f in range(5)]
+    loads = [pltpu.make_async_copy(sources[f], block.at[:, pl.ds(f * n_x, n_x)], sems.at[f]) for f in (4, 0, 1, 2)]
+    for first, sem in ((0, 3), (n_rows - HALO, 6)):
+        rows = pl.ds(first, HALO)
+        loads.append(
+            pltpu.make_async_copy(sources[3].at[rows, :], block.at[rows, pl.ds(3 * n_x, n_x)], sems.at[sem])
+        )
     for load in (*loads, off_load):
         load.start()
     line[...] = jnp.zeros_like(line)
@@ -463,7 +468,7 @@
             pltpu.VMEM((n_rows, wide), f32),
             pltpu.VMEM(offsets_x.shape, jnp.int32),
             pltpu.VMEM((1, LANES), f32),
-            pltpu.SemaphoreType.DMA((6,)),
+            pltpu.SemaphoreType.DMA((7,)),
             pltpu.SemaphoreType.DMA((3,)),
         ],
         compiler_params=pltpu.CompilerParams(vmem_limit_bytes=A_LIMIT),

time: 35.9 us -> 35.8 us (level)
  no operation moved by 1% of the time
where the time goes in v4:
time: 35.8 us; the launch traced here: 35.6 us
  starting transfers between devices  18 us (50%)
  Pallas kernels  7.62 us (21%)
  waiting for transfers between devices  5.17 us (14%)
  local copies, waits for them, and re-layouts  4.14 us (12%)
  between operations  0.66 us (2%)
    all_to_all x1, starting transfers between devices, body(): lax.all_to_all(pay, ('rows', 'cols'), split_axis=0, concat_axis=0, tiled=...  15.7 us
    all_to_all x1, waiting for transfers between devices, body(): lax.all_to_all(pay, ('rows', 'cols'), split_axis=0, concat_axis=0, tiled=...  4.34 us
    pallas_call x1, Pallas kernels, body(): pl.pallas_call(sweep_kernel, out_shape=(plane, jax.ShapeDtypeStruct(veloc...  4.23 us
    unnamed x10, local copies, waits for them, and re-layouts  4.14 us
    pallas_call x1, Pallas kernels, body(): pl.pallas_call(speed_kernel, out_shape=(jax.ShapeDtypeStruct((everyone, L...  2 us
    ppermute x1, starting transfers between devices, body(): lax.ppermute(up, 'rows', [(i, (i + 1) % n_dev) for i in range(n_dev)])  1.83 us
    ppermute x1, waiting for transfers between devices, body(): lax.ppermute(down, 'rows', [(i, (i - 1) % n_dev) for i in range(n_dev)])  0.83 us
    pallas_call x1, Pallas kernels, body(): pl.pallas_call(own_kernel, out_shape=(jax.ShapeDtypeStruct((9, n_own * SU...  0.78 us
  transfers between devices with their start and end apart: 3, of which 2 were waited for; matrix products, arithmetic and copies ran while one was open for 0% of the time, Pallas kernels for 4%

profile of v4, /device:TPU:1, one launch (start us, length us, event | category | flops | bytes accessed | tf_op | source)
XLA Modules:
  0.0 35.6 jit_solution(8570366481585207442)
XLA Ops:
  0.6 2.0 %shard_map.77 = (f32[256,128]{1,0:T(8,128)}, f32[8,5248]{1,0:T(8,128)}, f32[8,5248]{1,0:T(8,128)}) custom-call(f32[1,32,1024]{2,1,0:T(8,128)} %den.3, f32[3,1,32,1024]{3,2,1,0:T(8,128)} %vel.3, f32[1,32,1024]{2,1,0:T(8,128)} %prs.3, s32[1,32]{1,0:T(1,128)} %offx_hbm.1), custom_call_target="tpu_custom_call" | custom-call | tf_op jit(solution)/shard_map/pallas_call | solution.py:461
  2.6 15.7 %all-to-all-start = ((f32[256,1,128]{2,1,0:T(1,128)}), f32[256,1,128]{2,1,0:T(1,128)S(1)}, u32[]{:S(2)}, u32[]{:S(2)}) async-start(f32[256,1,128]{2,1,0:T(1,128)} %bitcast.5), calls=%async_computation | async-start | bytes 262144 | tf_op jit(solution)/shard_map/all_to_all | solution.py:476
  18.3 1.8 %collective-permute-start = (f32[8,5248]{1,0:T(8,128)}, f32[8,5248]{1,0:T(8,128)S(1)}, u32[]{:S(2)}, u32[]{:S(2)}) collective-permute-start(f32[8,5248]{1,0:T(8,128)} %get-tuple-element.12), channel_id=1, source_target_pairs={{0,8},{8,16},{16,24},{24,32},{32,40},{40,48},{48,56},{56,64},{64,7... | collective-permute-start | bytes 503816 | tf_op jit(solution)/shard_map/ppermute | solution.py:477
  20.1 0.5 %collective-permute-start.1 = (f32[8,5248]{1,0:T(8,128)}, f32[8,5248]{1,0:T(8,128)S(1)}, u32[]{:S(2)}, u32[]{:S(2)}) collective-permute-start(f32[8,5248]{1,0:T(8,128)} %get-tuple-element.13), channel_id=1, source_target_pairs={{0,248},{8,0},{16,8},{24,16},{32,24},{40,32},{48,40},{56,48},{64,5... | collective-permute-start | bytes 503816 | tf_op jit(solution)/shard_map/ppermute | solution.py:478
  20.6 0.0 copy-start
  20.6 1.0 %copy-done = f32[3,1,32,1024]{3,2,1,0:T(8,128)S(1)} copy-done((f32[3,1,32,1024]{3,2,1,0:T(8,128)S(1)}, f32[3,1,32,1024]{3,2,1,0:T(8,128)}, u32[]{:S(2)}) %copy-start) | copy-done | bytes 393240
  21.6 0.0 copy-start.1
  21.6 0.9 %copy-done.1 = f32[1,32,1024]{2,1,0:T(8,128)S(1)} copy-done((f32[1,32,1024]{2,1,0:T(8,128)S(1)}, f32[1,32,1024]{2,1,0:T(8,128)}, u32[]{:S(2)}) %copy-start.1) | copy-done | bytes 131096
  22.5 0.0 copy-start.2
  22.5 0.9 %copy-done.2 = f32[1,32,1024]{2,1,0:T(8,128)S(1)} copy-done((f32[1,32,1024]{2,1,0:T(8,128)S(1)}, f32[1,32,1024]{2,1,0:T(8,128)}, u32[]{:S(2)}) %copy-start.2) | copy-done | bytes 131096
  23.4 0.0 copy-start.3
  23.4 0.7 %copy-done.3 = s32[1,1024]{1,0:T(1,128)S(1)} copy-done((s32[1,1024]{1,0:T(1,128)S(1)}, s32[1,1024]{1,0:T(1,128)}, u32[]{:S(2)}) %copy-start.3) | copy-done | bytes 4120
  24.1 0.0 copy-start.4
  24.1 0.7 %copy-done.4 = s32[1,32]{1,0:T(1,128)S(1)} copy-done((s32[1,32]{1,0:T(1,128)S(1)}, s32[1,32]{1,0:T(1,128)}, u32[]{:S(2)}) %copy-start.4) | copy-done | bytes 152
  24.8 0.8 %shard_map.76 = (f32[9,16,2560]{2,1,0:T(8,128)S(1)}, f32[16,128]{1,0:T(8,128)S(1)}, f32[8,128]{1,0:T(8,128)S(1)}) custom-call(f32[1,32,1024]{2,1,0:T(8,128)S(1)} %copy-done.1, f32[3,1,32,1024]{3,2,1,0:T(8,128)S(1)} %copy-done, f32[1,32,1024]{2,1,0:T(8,128)S(1)} %copy-done.2, s32[1,32]{1,0:T(1,128)S(1)} %copy-done.4, s32[1,1024]{1,0:T(1,128)S(1)} %copy-done.3), custom_call_target="tpu_custom_call" | custom-call | flops 1000000 | bytes 1000000 | tf_op jit(solution)/shard_map/pallas_call | solution.py:482
  25.5 0.0 collective-permute-done.before
  25.6 0.8 %collective-permute-done.1.after = f32[8,5248]{1,0:T(8,128)S(1)} collective-permute-done((f32[8,5248]{1,0:T(8,128)}, f32[8,5248]{1,0:T(8,128)S(1)}, u32[]{:S(2)}, u32[]{:S(2)}) %collective-permute-start.1) | collective-permute-done | bytes 167968 | tf_op jit(solution)/shard_map/ppermute | solution.py:478
  26.4 0.6 %shard_map.78 = (f32[9,8,2560]{2,1,0:T(8,128)S(1)}, f32[8,128]{1,0:T(8,128)S(1)}) custom-call(f32[8,5248]{1,0:T(8,128)S(1)} %collective-permute-done.before, f32[8,5248]{1,0:T(8,128)S(1)} %collective-permute-done.1.after), custom_call_target="tpu_custom_call" | custom-call | flops 1000000 | bytes 1000000 | tf_op jit(solution)/shard_map/pallas_call | solution.py:495
  27.0 4.3 %all-to-all-done = f32[256,1,128]{2,1,0:T(1,128)S(1)} async-done(((f32[256,1,128]{2,1,0:T(1,128)}), f32[256,1,128]{2,1,0:T(1,128)S(1)}, u32[]{:S(2)}, u32[]{:S(2)}) %all-to-all-start) | async-done | bytes 131104 | tf_op jit(solution)/shard_map/all_to_all | solution.py:476
  31.3 4.2 %shard_map.79 = (f32[1,32,1024]{2,1,0:T(8,128)}, f32[3,1,32,1024]{3,2,1,0:T(8,128)}, f32[1,32,1024]{2,1,0:T(8,128)}) custom-call(f32[9,16,2560]{2,1,0:T(8,128)S(1)} %get-tuple-element.11.state, f32[9,8,2560]{2,1,0:T(8,128)S(1)} %get-tuple-element.14.halo_state, f32[256,128]{1,0:T(8,128)S(1)} %bitcast.4, f32[16,128]{1,0:T(8,128)S(1)} %get-tuple-element.16.rows_by, ...), custom_call_target="tpu_custom_call" | custom-call | tf_op jit(solution)/shard_map/pallas_call | solution.py:509
Async XLA Ops:
  2.6 28.7 %all-to-all-start = ((f32[256,1,128]{2,1,0:T(1,128)}), f32[256,1,128]{2,1,0:T(1,128)S(1)}, u32[]{:S(2)}, u32[]{:S(2)}) async-start(f32[256,1,128]{2,1,0:T(1,128)} %bitcast.5), calls=%async_computation | async-start | bytes 262144 | tf_op jit(solution)/shard_map/all_to_all | solution.py:476
  18.3 7.2 %collective-permute-start = (f32[8,5248]{1,0:T(8,128)}, f32[8,5248]{1,0:T(8,128)S(1)}, u32[]{:S(2)}, u32[]{:S(2)}) collective-permute-start(f32[8,5248]{1,0:T(8,128)} %get-tuple-element.12), channel_id=1, source_target_pairs={{0,8},{8,16},{16,24},{24,32},{32,40},{40,48},{48,56},{56,64},{64,7... | collective-permute-start | bytes 503816 | tf_op jit(solution)/shard_map/ppermute | solution.py:477
  20.1 6.2 %collective-permute-start.1 = (f32[8,5248]{1,0:T(8,128)}, f32[8,5248]{1,0:T(8,128)S(1)}, u32[]{:S(2)}, u32[]{:S(2)}) collective-permute-start(f32[8,5248]{1,0:T(8,128)} %get-tuple-element.13), channel_id=1, source_target_pairs={{0,248},{8,0},{16,8},{24,16},{32,24},{40,32},{48,40},{56,48},{64,5... | collective-permute-start | bytes 503816 | tf_op jit(solution)/shard_map/ppermute | solution.py:478
  20.6 1.0 %copy-start = (f32[3,1,32,1024]{3,2,1,0:T(8,128)S(1)}, f32[3,1,32,1024]{3,2,1,0:T(8,128)}, u32[]{:S(2)}) copy-start(f32[3,1,32,1024]{3,2,1,0:T(8,128)} %vel.3) | copy-start | bytes 1179652
  21.6 0.9 %copy-start.1 = (f32[1,32,1024]{2,1,0:T(8,128)S(1)}, f32[1,32,1024]{2,1,0:T(8,128)}, u32[]{:S(2)}) copy-start(f32[1,32,1024]{2,1,0:T(8,128)} %den.3) | copy-start | bytes 393220
  22.5 0.9 %copy-start.2 = (f32[1,32,1024]{2,1,0:T(8,128)S(1)}, f32[1,32,1024]{2,1,0:T(8,128)}, u32[]{:S(2)}) copy-start(f32[1,32,1024]{2,1,0:T(8,128)} %prs.3) | copy-start | bytes 393220
  23.4 0.7 %copy-start.3 = (s32[1,1024]{1,0:T(1,128)S(1)}, s32[1,1024]{1,0:T(1,128)}, u32[]{:S(2)}) copy-start(s32[1,1024]{1,0:T(1,128)} %offy.1) | copy-start | bytes 12292
  24.1 0.7 %copy-start.4 = (s32[1,32]{1,0:T(1,128)S(1)}, s32[1,32]{1,0:T(1,128)}, u32[]{:S(2)}) copy-start(s32[1,32]{1,0:T(1,128)} %offx_hbm.1) | copy-start | bytes 388
